TPU v7x, 32 devices: a whole 2x2x4 slice. The times are simulated.
32 devices in a mesh: owner: 4 (over x, core), fsdp: 8 (over z, y).
Axes of the slice: x: 2, y: 2, z: 4, core: 2. Of those that a mesh axis runs over, the one named last changes fastest.
Arguments:
- precond: bfloat16 [4, 2048, 2048], P('owner', 'fsdp'), as said below
- basis_old: bfloat16 [4, 2048, 2048], P('owner', 'fsdp'), as said below
- gradient: bfloat16 [8192, 8192], P('owner', 'fsdp'), may hold values from -6 to 6
- moment_in: float32 [8192, 8192], P('owner', 'fsdp')
- second_in: float32 [8192, 8192], P('owner', 'fsdp'), may hold values from 0.3 to 3
Outputs:
- update: bfloat16 [8192, 8192], P('owner', 'fsdp')
- moment_one: float32 [8192, 8192], P('owner', 'fsdp')
- moment_two: float32 [8192, 8192], P('owner', 'fsdp')
- basis_new: float32 [4, 2048, 2048], P('owner', 'fsdp')
Inputs may be any that keep to these rules, and one draw needn't show every extreme that they name: Each block of precond is symmetric and positive definite. Each block of basis_old is invertible.
All inputs are finite; a program needn't handle non-finite values.
Results may differ from a plain program's by a relative error of at most 0.024.
Values may be sent and summed in bfloat16 or wider, within the bound.
A program may use at most 192 MiB of HBM per device.

v0:
```python
import jax
import jax.numpy as jnp
from jax import lax
from jax.sharding import PartitionSpec as P

beta_one = 0.9
beta_two = 0.95
small_eps = 1e-08
norm_eps = 1e-06


def pack_gram(full, half):
    top = full[:, :half, half:]
    mixed = jnp.triu(full[:, :half, :half]) + jnp.tril(full[:, half:, half:], -1)
    diagonal = jnp.diagonal(full[:, half:, half:], axis1=1, axis2=2)
    return (jnp.stack([top, mixed], axis=1), diagonal)


def unpack_gram(packed, diagonal, half):
    top = packed[:, 0]
    mixed = packed[:, 1]
    corner = jnp.triu(mixed) + jnp.swapaxes(jnp.triu(mixed, 1), 1, 2)
    strict = jnp.tril(mixed, -1)
    lower = (
        strict
        + jnp.swapaxes(strict, 1, 2)
        + diagonal[:, :, None] * jnp.eye(half, dtype=jnp.float32)[None]
    )
    upper_band = jnp.concatenate([corner, top], axis=2)
    lower_band = jnp.concatenate([jnp.swapaxes(top, 1, 2), lower], axis=2)
    return jnp.concatenate([upper_band, lower_band], axis=1)


def orthonormal(chol, power):

    def solve_one(factor, rows):
        return jax.scipy.linalg.solve_triangular(factor, rows.T, lower=True).T

    return jax.vmap(solve_one)(chol, power)


def on_device(precond, basis_old, gradient, moment_in, second_in):
    blocks = precond.shape[0]
    order = precond.shape[2]
    half = order // 2
    width = gradient.shape[1]
    power = jnp.einsum(
        "bik,bkj->bij",
        precond,
        lax.all_gather(basis_old, "fsdp", axis=1, tiled=True),
        preferred_element_type=jnp.float32,
    )
    power_half = power.astype(jnp.bfloat16)
    partial_gram = jnp.einsum(
        "bki,bkj->bij", power_half, power_half, preferred_element_type=jnp.float32
    )
    packed, diagonal = pack_gram(partial_gram, half)
    packed_sum, diagonal_sum = lax.psum((packed, diagonal), "fsdp")
    gram_sum = unpack_gram(packed_sum, diagonal_sum, half)
    chol = jnp.linalg.cholesky(gram_sum)
    basis_new = orthonormal(chol, power_half.astype(jnp.float32))
    basis_half = basis_new.astype(jnp.bfloat16)
    moment_one = beta_one * moment_in + (1.0 - beta_one) * gradient.astype(jnp.float32)
    moment_half = moment_one.astype(jnp.bfloat16)
    gradient_block_list = gradient.reshape(blocks, order, width)
    moment_block_list = moment_half.reshape(blocks, order, width)
    complete_basis = lax.all_gather(basis_half, "fsdp", axis=1, tiled=True)
    rotated_gradient = jnp.einsum(
        "aos,aol->asl", complete_basis, gradient_block_list, preferred_element_type=jnp.float32
    )
    rotated_moment = jnp.einsum(
        "aos,aol->asl", complete_basis, moment_block_list, preferred_element_type=jnp.float32
    )
    moment_two = beta_two * second_in.reshape(blocks, order, width) + (1.0 - beta_two) * jnp.square(
        rotated_gradient
    )
    step_ratio = (rotated_moment / (jnp.sqrt(moment_two) + small_eps)).astype(jnp.bfloat16)
    unscaled_update = jnp.einsum(
        "rfu,rup->rfp", complete_basis, step_ratio, preferred_element_type=jnp.float32
    )
    total = lax.psum(jnp.sum(unscaled_update * unscaled_update), ("owner", "fsdp"))
    count = gradient.shape[0] * lax.axis_size("owner") * width * lax.axis_size("fsdp")
    scale = jnp.sqrt(jnp.float32(count)) / (jnp.sqrt(total) + norm_eps)
    update = (unscaled_update * scale).reshape(blocks * order, width).astype(jnp.bfloat16)
    return (update, moment_one, moment_two.reshape(blocks * order, width), basis_new)


def solution(mesh):
    return jax.shard_map(
        on_device,
        mesh=mesh,
        in_specs=(
            P("owner", "fsdp", None),
            P("owner", "fsdp", None),
            P("owner", "fsdp"),
            P("owner", "fsdp"),
            P("owner", "fsdp"),
        ),
        out_specs=(
            P("owner", "fsdp"),
            P("owner", "fsdp"),
            P("owner", "fsdp"),
            P("owner", "fsdp", None),
        ),
        check_vma=False,
    )
```

profile of v0, /device:TPU:0, one launch (start us, length us, event | category | flops | bytes accessed | tf_op | source)
XLA Modules:
  0.0 1502.7 jit_solution(8910131469121555497)
XLA Ops:
  8.0 129.8 %all-gather.3.cloned.1.call-done = bf16[1,2048,2048]{2,1,0:T(8,128)(2,1)} async-done(((bf16[1,256,2048]{2,1,0:T(8,128)(2,1)}), bf16[1,2048,2048]{2,1,0:T(8,128)(2,1)}) %all-gather.3.cloned.1.call-update) | async-done | bytes 8388624 | tf_op jit(solution)/shard_map/all_gather | solution.py:50
  157.5 17.3 %gather_fusion = f32[1024]{0:T(1024)S(1)} fusion(f32[1024,1024]{1,0:T(8,128)} %get-tuple-element.30, s32[1024]{0:T(1024)S(1)} %bitcast.844), kind=kCustom, calls=%fused_computation | custom fusion | bytes 16384 | tf_op jit(solution)/shard_map/jit(diagonal)/gather | solution.py:15
  174.8 19.8 %psum.25 = f32[1024]{0:T(1024)S(1)} all-reduce(f32[1024]{0:T(1024)S(1)} %gather_fusion), channel_id=1, replica_groups=mesh['owner'=4,'fsdp'=8] {'fsdp'}, use_global_device_ids=true, to_apply=%region_1.2 | all-reduce | flops 1024 | bytes 8192 | tf_op jit(solution)/shard_map/psum | solution.py:58
  194.6 229.2 %all-reduce.3.cloned.1.call-done = f32[1,2,1024,1024]{3,2,1,0:T(8,128)} async-done(((f32[1,2,1024,1024]{3,2,1,0:T(8,128)}), f32[1,2,1024,1024]{3,2,1,0:T(8,128)}) %all-reduce.3.cloned.1.call-update) | async-done | bytes 8388624 | tf_op jit(solution)/shard_map/psum | solution.py:58
  423.7 9.5 slice_bitcast_fusion.8
  452.5 9.2 copy.41
  479.3 13.2 maximum_maximum_fusion
  492.5 17.6 %copy.42 = f32[1,2048,2048]{2,1,0:T(8,128)} copy(f32[1,2048,2048]{1,2,0:T(8,128)} %maximum_maximum_fusion) | data formatting | bytes 33554432 | tf_op jit(solution)/shard_map/concatenate | solution.py:31
  510.1 13.6 fusion
  529.4 11.7 custom-call.143
  541.2 9.8 custom-call.144
  564.1 11.9 custom-call.145
  576.6 9.8 custom-call.146
  591.7 11.7 custom-call.147
  604.7 9.8 custom-call.148
  620.9 11.7 custom-call.149
  633.9 9.8 custom-call.150
  650.6 11.7 custom-call.151
  663.7 9.8 custom-call.152
  680.5 11.9 custom-call.153
  693.7 9.8 custom-call.154
  710.7 11.7 custom-call.155
  723.8 10.0 custom-call.156
  741.3 11.7 custom-call.157
  754.3 10.2 custom-call.158
  771.8 11.7 custom-call.159
  784.8 9.8 custom-call.160
  802.1 11.7 custom-call.161
  815.0 9.8 custom-call.162
  831.9 11.7 custom-call.163
  844.9 9.8 custom-call.164
  861.2 12.1 custom-call.165
  874.5 9.8 custom-call.166
  890.2 11.7 custom-call.167
  903.3 9.9 custom-call.168
  918.4 11.7 custom-call.169
  931.4 9.8 custom-call.170
  945.5 12.1 custom-call.171
  959.0 9.8 custom-call.172
  972.3 11.7 custom-call.173
  995.7 12.5 select_select_fusion
  1008.2 56.0 %while.1 = (s32[]{:T(128)}, f32[1,2048,2048]{2,1,0:T(8,128)}, s32[16,2]{0,1:T(2,128)S(1)}, f32[16,1,128,128]{3,2,1,0:T(8,128)}, s32[]{:T(128)}) while((s32[]{:T(128)}, f32[1,2048,2048]{2,1,0:T(8,128)}, s32[16,2]{0,1:T(2,128)S(1)}, f32[16,1,128,128]{3,2,1,0:T(8,128)}, s32[]{:T(128)}) %tuple.177), condition=%wide.while_cond, body=%wide.while_body.sunk | while | flops 2 | bytes 132705 | solution.py:37
  1064.3 158.8 %custom-call.174 = f32[1,16,128,128]{2,3,1,0:T(8,128)} custom-call(f32[1,16,128,128]{3,2,1,0:T(8,128)} %bitcast.852), custom_call_target="InvertDiagBlocksLowerTriangular" | custom-call | tf_op jit(solution)/shard_map/vmap(jit(_solve_triangular))/triangular_solve | solution.py:37
  1275.9 10.3 multiply_add_fusion.1
  1288.0 112.5 %all-gather.5.cloned.1.call-done = bf16[1,2048,2048]{1,2,0:T(8,128)(2,1)} async-done(((bf16[1,256,2048]{1,2,0:T(8,128)(2,1)}), bf16[1,2048,2048]{1,2,0:T(8,128)(2,1)}) %all-gather.5.cloned.1.call-update) | async-done | bytes 8388624 | tf_op jit(solution)/shard_map/all_gather | solution.py:67
  1400.5 16.1 %multiply_add_fusion = f32[2048,1024]{1,0:T(8,128)} fusion(f32[2048,1024]{1,0:T(8,128)} %param.9, bf16[2048,1024]{1,0:T(8,128)(2,1)} %param.7, bf16[1,2048,2048]{1,2,0:T(8,128)(2,1)} %all-gather.5.cloned.1.call-done), kind=kOutput, calls=%fused_computation.22 | convolution fusion | flops 8598323200 | bytes 29360128 | tf_op jit(solution)/shard_map/aos,aol->asl/dot_general | solution.py:68
  1416.6 33.3 %multiply_reduce_fusion = (f32[]{:T(128)}, f32[2048,1024]{1,0:T(8,128)}) fusion(f32[2048,1024]{1,0:T(8,128)} %multiply_add_fusion, f32[2048,1024]{1,0:T(8,128)} %multiply_add_fusion.1, bf16[1,2048,2048]{1,2,0:T(8,128)(2,1)} %all-gather.5.cloned.1.call-done), kind=kOutput, calls=%fused_computation.20 | convolution fusion | flops 17192452096 | bytes 33554436 | tf_op jit(solution)/shard_map/rfu,rup->rfp/dot_general | solution.py:78
  1449.9 38.6 %psum.26 = f32[]{:T(128)} all-reduce(f32[]{:T(128)} %get-tuple-element.215), channel_id=1, replica_groups=mesh['owner'=4,'fsdp'=8] {'owner','fsdp'}, use_global_device_ids=true, to_apply=%region_35.36 | all-reduce | flops 1 | bytes 8 | tf_op jit(solution)/shard_map/psum | solution.py:81
  (201 shorter events, 300.1 us)
Async XLA Ops:
  7.2 130.7 %copy-start = (bf16[1,256,2048]{2,1,0:T(8,128)(2,1)S(1)}, bf16[1,256,2048]{2,1,0:T(8,128)(2,1)}, u32[]{:S(2)}) copy-start(bf16[1,256,2048]{2,1,0:T(8,128)(2,1)} %param.5) | copy-start | bytes 3145732
  7.2 130.6 %all-gather.3.cloned.1.call-start = ((), (), s32[]{:S(2)}) async-start(), calls=%async_computation | async-start | bytes 9437184 | tf_op jit(solution)/shard_map/all_gather | solution.py:50
  7.9 415.8 %all-reduce.3.cloned.1.call-start = ((), (), s32[]{:S(2)}) async-start(), calls=%async_computation.1 | async-start | bytes 16777216 | tf_op jit(solution)/shard_map/psum | solution.py:58
  144.9 2.4 copy-start.6
  154.8 1245.7 %all-gather.5.cloned.1.call-start = ((), (), s32[]{:S(2)}) async-start(), calls=%async_computation.2 | async-start | bytes 9437184 | tf_op jit(solution)/shard_map/all_gather | solution.py:67
  443.9 4.6 copy-start.5
  472.3 7.0 copy-start.3
  477.3 2.0 copy-start.4
  523.7 5.7 copy-start.2
  1223.1 5.7 copy-start.8
  1225.7 5.7 copy-start.7
  1489.2 6.8 copy-start.1
Sparse Core Ops, SparseCore 0:
  10.1 127.6 all-gather.2
  154.9 268.8 all-reduce.2
  1276.0 124.4 all-gather.4
where the time goes:
time: 1510 us; the launch traced here: 1500 us
  other arithmetic  598 us (40%)
  waiting for transfers between devices  472 us (31%)
  matrix products  203 us (13%)
  local copies, waits for them, and re-layouts  145 us (10%)
  blocking collectives  58.4 us (4%)
  between operations  25.2 us (2%)
    another operation x62, other arithmetic, on_device(): chol = jnp.linalg.cholesky(gram_sum)  356 us
    psum x1, waiting for transfers between devices, on_device(): packed_sum, diagonal_sum = lax.psum((packed, diagonal), 'fsdp')  229 us
    another operation x3, other arithmetic, solve_one(): return jax.scipy.linalg.solve_triangular(factor, rows.T, lower=True).T  171 us
    all_gather x1, waiting for transfers between devices, on_device(): lax.all_gather(basis_old, 'fsdp', axis=1, tiled=True)  130 us
    all_gather x1, waiting for transfers between devices, on_device(): complete_basis = lax.all_gather(basis_half, 'fsdp', axis=1, tiled=True)  112 us
    another operation x30, matrix products, on_device(): chol = jnp.linalg.cholesky(gram_sum)  92.4 us
    another operation x48, local copies, waits for them, and re-layouts  56 us
    another operation x31, matrix products, solve_one(): return jax.scipy.linalg.solve_triangular(factor, rows.T, lower=True).T  51.5 us
  transfers between devices with their start and end apart: 3, of which 3 were waited for; matrix products, arithmetic and copies ran while one was open for 2% of the time, Pallas kernels for 0%

commit v1 on v0

v1 whole, which is shorter than its diff:
```python
import functools
import jax
import jax.numpy as jnp
from jax import lax
from jax.experimental import pallas as pl
from jax.experimental.pallas import tpu as pltpu
from jax.sharding import PartitionSpec as P

beta_one = 0.9
beta_two = 0.95
small_eps = 1e-08
norm_eps = 1e-06
TILE = 256
HALF = 128


def split(value):
    high = value.astype(jnp.bfloat16)
    return high, (value - high.astype(jnp.float32)).astype(jnp.bfloat16)


def dot(left, right, across):
    return lax.dot_general(
        left, right, (((1,), (across,)), ((), ())), preferred_element_type=jnp.float32
    )


def dot3(left, right, across):
    left_high, left_low = left
    right_high, right_low = right
    return (
        dot(left_high, right_low, across)
        + dot(left_low, right_high, across)
        + dot(left_high, right_high, across)
    )


def inverse_factor(square):
    groups = HALF // 8
    rows = [square[8 * g : 8 * g + 8, :] for g in range(groups)]
    lane = lax.broadcasted_iota(jnp.int32, (8, HALF), 1)
    sub = lax.broadcasted_iota(jnp.int32, (8, HALF), 0)
    result = []
    for q in range(groups):
        first = 8 * q
        in_panel = (lane >= first) & (lane < first + 8)

        def columns(g):
            return [
                jnp.broadcast_to(rows[g][:, first + i : first + i + 1], (8, HALF)) for i in range(8)
            ]

        panel = columns(q)
        top = jnp.where(in_panel, jnp.where(lane - first == sub, 1.0, 0.0), rows[q])
        scale = jnp.zeros((8, HALF), jnp.float32)
        inverses, pivots, links = [], [], []
        for i in range(8):
            pivot = jnp.broadcast_to(panel[i][i : i + 1, :], (8, HALF))
            inverse = 1.0 / pivot
            factor = jnp.where(sub > i, panel[i] * inverse, 0.0)
            pivot_row = jnp.broadcast_to(top[i : i + 1, :], (8, HALF))
            link = {}
            for later in range(i + 1, 8):
                link[later] = jnp.broadcast_to(panel[later][i : i + 1, :], (8, HALF))
                panel[later] = panel[later] - factor * link[later]
            top = top - factor * pivot_row
            scale = jnp.where(sub == i, lax.rsqrt(pivot), scale)
            inverses.append(inverse)
            pivots.append(pivot_row)
            links.append(link)
        result.append(jnp.where(lane < first + 8, top * scale, 0.0))
        for g in range(q + 1, groups):
            below = columns(g)
            value = jnp.where(in_panel, 0.0, rows[g])
            for i in range(8):
                factor = below[i] * inverses[i]
                for later in range(i + 1, 8):
                    below[later] = below[later] - factor * links[i][later]
                value = value - factor * pivots[i]
            rows[g] = value
    return jnp.concatenate(result, axis=0)


def factor_kernel(
    count, gram_ref, inv_high, inv_low, low_high, low_low, diag_ref, side_ref, wide_high, wide_low
):
    def tile(index):
        return pl.ds(pl.multiple_of(index * TILE, TILE), TILE)

    def lower(i, k):
        return low_high[tile(i), tile(k)], low_low[tile(i), tile(k)]

    @pl.loop(0, count)
    def _(i):
        inv_high[tile(i), :] = jnp.zeros((TILE, count * TILE), jnp.bfloat16)
        inv_low[tile(i), :] = jnp.zeros((TILE, count * TILE), jnp.bfloat16)

    @pl.loop(0, count)
    def _(j):
        def column(i):
            def step(k, total):
                return total - dot3(lower(i, k), lower(j, k), 1)

            return lax.fori_loop(0, j, step, gram_ref[tile(i), tile(j)])

        diag_ref[...] = column(j)

        @pl.loop(0, 2)
        def _(h):
            part = pl.ds(pl.multiple_of(h * HALF, HALF), HALF)
            inverse = inverse_factor(diag_ref[part, part])
            high, low = split(inverse)
            wide_high[part, part] = high
            wide_low[part, part] = low

            @pl.when(h == 0)
            def _():
                side = dot3(split(diag_ref[HALF:, :HALF]), (high, low), 1)
                pair = split(side)
                side_ref[...] = side
                diag_ref[HALF:, HALF:] = diag_ref[HALF:, HALF:] - dot3(pair, pair, 1)
                wide_high[:HALF, HALF:] = jnp.zeros((HALF, HALF), jnp.bfloat16)
                wide_low[:HALF, HALF:] = jnp.zeros((HALF, HALF), jnp.bfloat16)

            @pl.when(h == 1)
            def _():
                first = wide_high[:HALF, :HALF], wide_low[:HALF, :HALF]
                corner = dot3(split(side_ref[...]), first, 0)
                corner_high, corner_low = split(-dot3((high, low), split(corner), 0))
                wide_high[HALF:, :HALF] = corner_high
                wide_low[HALF:, :HALF] = corner_low

        def wide():
            return wide_high[...], wide_low[...]

        @pl.loop(j + 1, count)
        def _(i):
            high, low = split(dot3(split(column(i)), wide(), 1))
            low_high[tile(i), tile(j)] = high
            low_low[tile(i), tile(j)] = low

        @pl.loop(0, j)
        def _(c):
            def step(k, total):
                return total + dot3(lower(j, k), (inv_high[tile(k), tile(c)], inv_low[tile(k), tile(c)]), 0)

            total = lax.fori_loop(c, j, step, jnp.zeros((TILE, TILE), jnp.float32))
            high, low = split(-dot3(wide(), split(total), 0))
            inv_high[tile(j), tile(c)] = high
            inv_low[tile(j), tile(c)] = low

        inv_high[tile(j), tile(j)] = wide_high[...]
        inv_low[tile(j), tile(j)] = wide_low[...]


def inverse_of_factor(gram):
    order = gram.shape[0]
    whole = jax.ShapeDtypeStruct((order, order), jnp.bfloat16)
    return pl.pallas_call(
        functools.partial(factor_kernel, order // TILE),
        out_shape=(whole, whole),
        in_specs=[pl.BlockSpec(memory_space=pltpu.VMEM)],
        out_specs=(pl.BlockSpec(memory_space=pltpu.VMEM), pl.BlockSpec(memory_space=pltpu.VMEM)),
        scratch_shapes=[
            pltpu.VMEM((order, order), jnp.bfloat16),
            pltpu.VMEM((order, order), jnp.bfloat16),
            pltpu.VMEM((TILE, TILE), jnp.float32),
            pltpu.VMEM((HALF, HALF), jnp.float32),
            pltpu.VMEM((TILE, TILE), jnp.bfloat16),
            pltpu.VMEM((TILE, TILE), jnp.bfloat16),
        ],
        compiler_params=pltpu.CompilerParams(vmem_limit_bytes=58 * 1024 * 1024),
    )(gram)


def rotate(rows, inverse):
    high, low = inverse
    return dot(rows, low, 1) + dot(rows, high, 1)


def on_device(precond, basis_old, gradient, moment_in, second_in):
    blocks = precond.shape[0]
    order = precond.shape[2]
    width = gradient.shape[1]
    power = jnp.einsum(
        "bik,bkj->bij",
        precond,
        lax.all_gather(basis_old, "fsdp", axis=1, tiled=True),
        preferred_element_type=jnp.float32,
    )
    power_half = power.astype(jnp.bfloat16)
    complete_power = lax.all_gather(power_half, "fsdp", axis=1, tiled=True)
    gram_sum = jnp.einsum(
        "bki,bkj->bij", complete_power, complete_power, preferred_element_type=jnp.float32
    )
    inverses = [inverse_of_factor(gram_sum[b]) for b in range(blocks)]
    basis_new = jnp.stack([rotate(power_half[b], inverses[b]) for b in range(blocks)])
    complete_basis = jnp.stack(
        [rotate(complete_power[b], inverses[b]).astype(jnp.bfloat16) for b in range(blocks)]
    )
    moment_one = beta_one * moment_in + (1.0 - beta_one) * gradient.astype(jnp.float32)
    moment_half = moment_one.astype(jnp.bfloat16)
    gradient_block_list = gradient.reshape(blocks, order, width)
    moment_block_list = moment_half.reshape(blocks, order, width)
    rotated_gradient = jnp.einsum(
        "aos,aol->asl", complete_basis, gradient_block_list, preferred_element_type=jnp.float32
    )
    rotated_moment = jnp.einsum(
        "aos,aol->asl", complete_basis, moment_block_list, preferred_element_type=jnp.float32
    )
    moment_two = beta_two * second_in.reshape(blocks, order, width) + (1.0 - beta_two) * jnp.square(
        rotated_gradient
    )
    step_ratio = (rotated_moment / (jnp.sqrt(moment_two) + small_eps)).astype(jnp.bfloat16)
    unscaled_update = jnp.einsum(
        "rfu,rup->rfp", complete_basis, step_ratio, preferred_element_type=jnp.float32
    )
    total = lax.psum(jnp.sum(unscaled_update * unscaled_update), ("owner", "fsdp"))
    count = gradient.shape[0] * lax.axis_size("owner") * width * lax.axis_size("fsdp")
    scale = jnp.sqrt(jnp.float32(count)) / (jnp.sqrt(total) + norm_eps)
    update = (unscaled_update * scale).reshape(blocks * order, width).astype(jnp.bfloat16)
    return (update, moment_one, moment_two.reshape(blocks * order, width), basis_new)


def solution(mesh):
    return jax.shard_map(
        on_device,
        mesh=mesh,
        in_specs=(
            P("owner", "fsdp", None),
            P("owner", "fsdp", None),
            P("owner", "fsdp"),
            P("owner", "fsdp"),
            P("owner", "fsdp"),
        ),
        out_specs=(
            P("owner", "fsdp"),
            P("owner", "fsdp"),
            P("owner", "fsdp"),
            P("owner", "fsdp", None),
        ),
        check_vma=False,
    )
```

time: 1510 us -> 614 us (0.41)
  other arithmetic: 598 us -> 16.9 us
  waiting for transfers between devices: 472 us -> 244 us
  Pallas kernels: 0 us -> 152 us
  local copies, waits for them, and re-layouts: 145 us -> 0.03 us
  matrix products: 203 us -> 144 us
  blocking collectives: 58.4 us -> 38.8 us
    another operation x66 -> x0, other arithmetic: 532 us -> none  [the longest x62 356 us: on_device(): chol = jnp.linalg.cholesky(gram_sum)]
    psum x1 -> x0, waiting for transfers between devices: 229 us -> none  [on_device(): packed_sum, diagonal_sum = lax.psum((packed, diagonal), 'fsdp')]
    pallas_call x0 -> x1, Pallas kernels: none -> 152 us  [inverse_of_factor(): pl.pallas_call(functools.partial(factor_kernel, order // TILE), out_shape...]
    another operation x61 -> x0, matrix products: 144 us -> none  [the longest x30 92.4 us: on_device(): chol = jnp.linalg.cholesky(gram_sum)]
    dot_general x1 -> x5, matrix products: 2.38 us -> 86.9 us  [the longest x4 62.5 us: dot(): lax.dot_general(left, right, (((1,), (across,)), ((), ())), preferred_ele...]
    another operation x65 -> x0, local copies, waits for them, and re-layouts: 63.9 us -> none
    concatenate x2 -> x0, local copies, waits for them, and re-layouts: 26.8 us -> none  [the longest x1 17.6 us: unpack_gram(): return jnp.concatenate([upper_band, lower_band], axis=1)]
    psum x1 -> x0, blocking collectives: 19.8 us -> none  [on_device(): packed_sum, diagonal_sum = lax.psum((packed, diagonal), 'fsdp')]
  transfers between devices with their start and end apart: 3 -> 2, of which waited for: 3 -> 2; matrix products, arithmetic and copies ran while one was open for 2% -> 2% of each run, Pallas kernels for 0% -> 0%
where the time goes in v1:
time: 614 us; the launch traced here: 610 us
  waiting for transfers between devices  244 us (40%)
  Pallas kernels  152 us (25%)
  matrix products  144 us (23%)
  blocking collectives  38.8 us (6%)
  other arithmetic  16.9 us (3%)
  between operations  15 us (2%)
    pallas_call x1, Pallas kernels, inverse_of_factor(): pl.pallas_call(functools.partial(factor_kernel, order // TILE), out_shape...  152 us
    all_gather x1, waiting for transfers between devices, on_device(): lax.all_gather(basis_old, 'fsdp', axis=1, tiled=True)  130 us
    all_gather x1, waiting for transfers between devices, on_device(): complete_power = lax.all_gather(power_half, 'fsdp', axis=1, tiled=True)  113 us
    dot_general x4, matrix products, dot(): lax.dot_general(left, right, (((1,), (across,)), ((), ())), preferred_ele...  62.5 us
    psum x1, blocking collectives, on_device(): lax.psum(jnp.sum(unscaled_update * unscaled_update), ('owner', 'fsdp'))  38.8 us
    dot_general x1, matrix products, on_device(): jnp.einsum('rfu,rup->rfp', complete_basis, step_ratio, preferred_element_...  33.8 us
    dot_general x1, matrix products, on_device(): jnp.einsum('bki,bkj->bij', complete_power, complete_power, preferred_elem...  24.4 us
    dot_general x1, matrix products, on_device(): jnp.einsum('aos,aol->asl', complete_basis, gradient_block_list, preferred...  16.4 us
  transfers between devices with their start and end apart: 2, of which 2 were waited for; matrix products, arithmetic and copies ran while one was open for 2% of the time, Pallas kernels for 0%

profile of v1, /device:TPU:0, one launch (start us, length us, event | category | flops | bytes accessed | tf_op | source)
XLA Modules:
  0.0 610.4 jit_solution(16954766285000500814)
XLA Ops:
  7.2 0.0 copy-start
  7.2 0.0 all-gather.4.cloned.1.call-start
  7.2 0.7 all-gather.4.cloned.1.call-update
  7.9 0.0 all-gather.6.cloned.1.call-start
  8.0 129.8 %all-gather.4.cloned.1.call-done = bf16[1,2048,2048]{2,1,0:T(8,128)(2,1)} async-done(((bf16[1,256,2048]{2,1,0:T(8,128)(2,1)}), bf16[1,2048,2048]{2,1,0:T(8,128)(2,1)}) %all-gather.4.cloned.1.call-update) | async-done | bytes 8388624 | tf_op jit(solution)/shard_map/all_gather | solution.py:188
  137.8 0.0 copy-done
  137.8 6.7 %fusion.11 = bf16[256,2048]{1,0:T(8,128)(2,1)} fusion(bf16[1,2048,2048]{2,1,0:T(8,128)(2,1)} %all-gather.4.cloned.1.call-done, bf16[1,256,2048]{2,1,0:T(8,128)(2,1)S(1)} %copy-done), kind=kOutput, calls=%fused_computation.14 | convolution fusion | flops 2148007936 | bytes 10485760 | tf_op jit(solution)/shard_map/bik,bkj->bij/dot_general | solution.py:185
  144.5 0.0 all-gather.6.cloned.1.call-update
  144.5 10.3 %multiply_add_fusion.1 = f32[2048,1024]{1,0:T(8,128)} fusion(bf16[2048,1024]{1,0:T(8,128)(2,1)} %param.7, f32[2048,1024]{1,0:T(8,128)} %param.8), kind=kLoop, calls=%fused_computation.7 | loop fusion | flops 8388608 | bytes 20971520 | tf_op jit(solution)/shard_map/add | solution.py:201
  154.8 113.0 %all-gather.6.cloned.1.call-done = bf16[2048,2048]{1,0:T(8,128)(2,1)} async-done(((bf16[256,2048]{1,0:T(8,128)(2,1)}), bf16[2048,2048]{1,0:T(8,128)(2,1)}) %all-gather.6.cloned.1.call-update) | async-done | bytes 8388624 | tf_op jit(solution)/shard_map/all_gather | solution.py:192
  267.8 24.4 %fusion.18.gram_ref = f32[2048,2048]{1,0:T(8,128)} fusion(bf16[2048,2048]{1,0:T(8,128)(2,1)} %all-gather.6.cloned.1.call-done), kind=kOutput, calls=%fused_computation.17 | convolution fusion | flops 17179869184 | bytes 25165824 | tf_op jit(solution)/shard_map/bki,bkj->bij/dot_general | solution.py:193
  292.2 0.0 copy-start.2
  292.2 152.3 %shard_map.84 = (bf16[2048,2048]{1,0:T(8,128)(2,1)}, bf16[2048,2048]{1,0:T(8,128)(2,1)}) custom-call(f32[2048,2048]{1,0:T(8,128)} %fusion.18.gram_ref), custom_call_target="tpu_custom_call" | custom-call | tf_op jit(solution)/shard_map/pallas_call | solution.py:159
  444.5 0.0 copy-start.4
  444.5 0.0 copy-done.2
  444.5 7.2 %fusion.20 = f32[256,2048]{1,0:T(8,128)} fusion(bf16[256,2048]{1,0:T(8,128)(2,1)S(1)} %copy-done.2, bf16[2048,2048]{1,0:T(8,128)(2,1)} %get-tuple-element.6), kind=kOutput, calls=%fused_computation.19 | convolution fusion | flops 2147483648 | bytes 11534336 | tf_op jit(solution)/shard_map/dot_general | solution.py:23
  451.7 0.0 copy-done.4
  451.7 22.0 %fusion.19 = f32[2048,2048]{1,0:T(8,128)} fusion(bf16[2048,2048]{1,0:T(8,128)(2,1)S(1)} %copy-done.4, bf16[2048,2048]{1,0:T(8,128)(2,1)} %get-tuple-element.6), kind=kOutput, calls=%fused_computation.18 | convolution fusion | flops 17179869184 | bytes 33554432 | tf_op jit(solution)/shard_map/dot_general | solution.py:23
  473.8 25.4 %add_convert_fusion = bf16[2048,2048]{1,0:T(8,128)(2,1)} fusion(f32[2048,2048]{1,0:T(8,128)} %fusion.19, bf16[2048,2048]{1,0:T(8,128)(2,1)} %all-gather.6.cloned.1.call-done, bf16[2048,2048]{1,0:T(8,128)(2,1)} %get-tuple-element.7), kind=kOutput, calls=%fused_computation | convolution fusion | flops 17188257792 | bytes 41943040 | tf_op jit(solution)/shard_map/dot_general | solution.py:23
  499.2 16.4 %multiply_add_fusion = f32[2048,1024]{1,0:T(8,128)} fusion(f32[2048,1024]{1,0:T(8,128)} %param.9, bf16[2048,2048]{1,0:T(8,128)(2,1)} %add_convert_fusion, bf16[2048,1024]{1,0:T(8,128)(2,1)} %param.7), kind=kOutput, calls=%fused_computation.6 | convolution fusion | flops 8598323200 | bytes 29360128 | tf_op jit(solution)/shard_map/aos,aol->asl/dot_general | solution.py:205
  515.6 0.0 copy-start.3
  515.6 33.8 %multiply_reduce_fusion = (f32[]{:T(128)}, f32[2048,1024]{1,0:T(8,128)}) fusion(bf16[2048,2048]{1,0:T(8,128)(2,1)} %add_convert_fusion, f32[2048,1024]{1,0:T(8,128)} %multiply_add_fusion, f32[2048,1024]{1,0:T(8,128)} %multiply_add_fusion.1), kind=kOutput, calls=%fused_computation.4 | convolution fusion | flops 17192452096 | bytes 33554436 | tf_op jit(solution)/shard_map/rfu,rup->rfp/dot_general | solution.py:215
  549.4 38.8 %psum.7 = f32[]{:T(128)} all-reduce(f32[]{:T(128)} %get-tuple-element.8), channel_id=1, replica_groups=mesh['owner'=4,'fsdp'=8] {'owner','fsdp'}, use_global_device_ids=true, to_apply=%region_1.0 | all-reduce | flops 1 | bytes 8 | tf_op jit(solution)/shard_map/psum | solution.py:218
  588.9 0.0 copy-done.3
  588.9 0.0 copy-start.1
  588.9 7.8 %fusion.10 = f32[1,256,2048]{2,1,0:T(8,128)} fusion(f32[256,2048]{1,0:T(8,128)} %fusion.20, bf16[256,2048]{1,0:T(8,128)(2,1)S(1)} %copy-done.3, bf16[2048,2048]{1,0:T(8,128)(2,1)} %get-tuple-element.7), kind=kOutput, calls=%fused_computation.13 | convolution fusion | flops 2148007936 | bytes 13631488 | tf_op jit(solution)/shard_map/dot_general | solution.py:23
  596.7 6.7 %multiply_convert_fusion = bf16[2048,1024]{1,0:T(8,128)(2,1)} fusion(f32[2048,1024]{1,0:T(8,128)} %get-tuple-element.9, f32[]{:T(128)S(6)} %div.8), kind=kLoop, calls=%fused_computation.3 | loop fusion | flops 4194304 | bytes 12582916 | tf_op jit(solution)/shard_map/convert_element_type | solution.py:221
  603.4 0.0 copy-done.1
Async XLA Ops:
  7.2 130.6 %copy-start = (bf16[1,256,2048]{2,1,0:T(8,128)(2,1)S(1)}, bf16[1,256,2048]{2,1,0:T(8,128)(2,1)}, u32[]{:S(2)}) copy-start(bf16[1,256,2048]{2,1,0:T(8,128)(2,1)} %param.5) | copy-start | bytes 3145732
  7.2 130.6 %all-gather.4.cloned.1.call-start = ((), (), s32[]{:S(2)}) async-start(), calls=%async_computation | async-start | bytes 9437184 | tf_op jit(solution)/shard_map/all_gather | solution.py:188
  7.9 259.9 %all-gather.6.cloned.1.call-start = ((), (), s32[]{:S(2)}) async-start(), calls=%async_computation.1 | async-start | bytes 9437184 | tf_op jit(solution)/shard_map/all_gather | solution.py:192
  292.2 152.3 %copy-start.2 = (bf16[256,2048]{1,0:T(8,128)(2,1)S(1)}, bf16[256,2048]{1,0:T(8,128)(2,1)}, u32[]{:S(2)}) copy-start(bf16[256,2048]{1,0:T(8,128)(2,1)} %fusion.11) | copy-start | bytes 3145732
  444.5 7.2 %copy-start.4 = (bf16[2048,2048]{1,0:T(8,128)(2,1)S(1)}, bf16[2048,2048]{1,0:T(8,128)(2,1)}, u32[]{:S(2)}) copy-start(bf16[2048,2048]{1,0:T(8,128)(2,1)} %all-gather.6.cloned.1.call-done) | copy-start | bytes 25165828
  515.6 73.3 %copy-start.3 = (bf16[256,2048]{1,0:T(8,128)(2,1)S(1)}, bf16[256,2048]{1,0:T(8,128)(2,1)}, u32[]{:S(2)}) copy-start(bf16[256,2048]{1,0:T(8,128)(2,1)} %fusion.11) | copy-start | bytes 3145732
  588.9 14.5 %copy-start.1 = (bf16[1,256,2048]{2,1,0:T(8,128)(2,1)S(1)}, bf16[1,256,2048]{2,1,0:T(8,128)(2,1)}, u32[]{:S(2)}) copy-start(bf16[1,256,2048]{2,1,0:T(8,128)(2,1)} %param.5) | copy-start | bytes 3145732
Sparse Core Ops, SparseCore 0:
  10.1 127.6 all-gather.3
  144.6 123.1 all-gather.5

commit v2 on v1

--- a/solution.py
+++ b/solution.py
@@ -169,7 +169,10 @@
             pltpu.VMEM((TILE, TILE), jnp.bfloat16),
             pltpu.VMEM((TILE, TILE), jnp.bfloat16),
         ],
-        compiler_params=pltpu.CompilerParams(vmem_limit_bytes=58 * 1024 * 1024),
+        compiler_params=pltpu.CompilerParams(vmem_limit_bytes=40 * 1024 * 1024),
+        cost_estimate=pl.CostEstimate(
+            flops=60 * order**3, bytes_accessed=8 * order**2, transcendentals=0
+        ),
     )(gram)
 
 
@@ -178,26 +181,113 @@
     return dot(rows, low, 1) + dot(rows, high, 1)
 
 
+def gram_of(left, right):
+    return lax.dot_general(
+        left, right, (((0,), (0,)), ((), ())), preferred_element_type=jnp.float32
+    )
+
+
+def refresh(factor, first_basis, second_basis, start, count):
+    power_first = dot(factor, first_basis, 0).astype(jnp.bfloat16)
+    inverse_first = inverse_of_factor(gram_of(power_first, power_first))
+    basis_first = rotate(power_first, inverse_first).astype(jnp.bfloat16)
+    inverse_first, basis_first, second_basis = lax.optimization_barrier(
+        (inverse_first, basis_first, second_basis)
+    )
+    power_second = dot(factor, second_basis, 0).astype(jnp.bfloat16)
+    side = split(dot3(split(gram_of(power_second, power_first)), inverse_first, 1))
+    corner = gram_of(power_second, power_second) - dot3(side, side, 1)
+    inverse_second = inverse_of_factor(corner)
+    inverse_side = split(-dot3(inverse_second, split(dot3(side, inverse_first, 0)), 0))
+
+    def second_columns(first_rows, second_rows):
+        return rotate(first_rows, inverse_side) + rotate(second_rows, inverse_second)
+
+    basis_second = second_columns(power_first, power_second).astype(jnp.bfloat16)
+    own_first = lax.dynamic_slice_in_dim(power_first, start, count, 0)
+    own_second = lax.dynamic_slice_in_dim(power_second, start, count, 0)
+    own = [rotate(own_first, inverse_first), second_columns(own_first, own_second)]
+    return jnp.concatenate(own, axis=1), jnp.concatenate([basis_first, basis_second], axis=1)
+
+
+def sum_kernel(
+    owners, shards, value_ref, total_ref, near, far, middle, near_sent, near_come, far_sent, far_come
+):
+    me_owner, me_shard = lax.axis_index("owner"), lax.axis_index("fsdp")
+
+    def shard_at(step):
+        return {"owner": me_owner, "fsdp": lax.rem(me_shard + step, shards)}
+
+    def owner_at(step):
+        return {"owner": lax.rem(me_owner + step, owners), "fsdp": me_shard}
+
+    barrier = pltpu.get_barrier_semaphore()
+    peers = [shard_at(step) for step in range(1, shards)]
+    peers += [owner_at(step) for step in range(1, owners)]
+    for peer in peers:
+        pl.semaphore_signal(barrier, inc=1, device_id=peer, device_id_type=pl.DeviceIdType.MESH)
+    pl.semaphore_wait(barrier, shards + owners - 2)
+
+    def spread(source, boxes, sent, come, place, extent):
+        copies = [
+            pltpu.make_async_remote_copy(
+                src_ref=source,
+                dst_ref=boxes.at[step - 1],
+                send_sem=sent.at[step - 1],
+                recv_sem=come.at[step - 1],
+                device_id=place(step),
+                device_id_type=pl.DeviceIdType.MESH,
+            )
+            for step in range(1, extent)
+        ]
+        for copy in copies:
+            copy.start()
+        for copy in copies:
+            copy.wait()
+        total = source[...]
+        for step in range(1, extent):
+            total = total + boxes[step - 1]
+        return total
+
+    middle[...] = spread(value_ref, near, near_sent, near_come, shard_at, shards)
+    total_ref[...] = spread(middle, far, far_sent, far_come, owner_at, owners)
+
+
+def sum_everywhere(value):
+    owners, shards = lax.axis_size("owner"), lax.axis_size("fsdp")
+    shape = (8, 128)
+    total = pl.pallas_call(
+        functools.partial(sum_kernel, owners, shards),
+        out_shape=jax.ShapeDtypeStruct(shape, jnp.float32),
+        in_specs=[pl.BlockSpec(memory_space=pltpu.VMEM)],
+        out_specs=pl.BlockSpec(memory_space=pltpu.VMEM),
+        scratch_shapes=[
+            pltpu.VMEM((shards - 1,) + shape, jnp.float32),
+            pltpu.VMEM((owners - 1,) + shape, jnp.float32),
+            pltpu.VMEM(shape, jnp.float32),
+            pltpu.SemaphoreType.DMA((shards - 1,)),
+            pltpu.SemaphoreType.DMA((shards - 1,)),
+            pltpu.SemaphoreType.DMA((owners - 1,)),
+            pltpu.SemaphoreType.DMA((owners - 1,)),
+        ],
+        compiler_params=pltpu.CompilerParams(collective_id=0, has_side_effects=True),
+    )(jnp.broadcast_to(value, shape))
+    return total[0, 0]
+
+
 def on_device(precond, basis_old, gradient, moment_in, second_in):
-    blocks = precond.shape[0]
-    order = precond.shape[2]
+    blocks, held, order = precond.shape
     width = gradient.shape[1]
-    power = jnp.einsum(
-        "bik,bkj->bij",
-        precond,
-        lax.all_gather(basis_old, "fsdp", axis=1, tiled=True),
-        preferred_element_type=jnp.float32,
-    )
-    power_half = power.astype(jnp.bfloat16)
-    complete_power = lax.all_gather(power_half, "fsdp", axis=1, tiled=True)
-    gram_sum = jnp.einsum(
-        "bki,bkj->bij", complete_power, complete_power, preferred_element_type=jnp.float32
-    )
-    inverses = [inverse_of_factor(gram_sum[b]) for b in range(blocks)]
-    basis_new = jnp.stack([rotate(power_half[b], inverses[b]) for b in range(blocks)])
-    complete_basis = jnp.stack(
-        [rotate(complete_power[b], inverses[b]).astype(jnp.bfloat16) for b in range(blocks)]
-    )
+    half = order // 2
+    start = lax.axis_index("fsdp") * held
+    factor = lax.all_gather(precond, "fsdp", axis=1, tiled=True)
+    first_basis = lax.all_gather(basis_old[:, :, :half], "fsdp", axis=1, tiled=True)
+    second_basis = lax.all_gather(basis_old[:, :, half:], "fsdp", axis=1, tiled=True)
+    refreshed = [
+        refresh(factor[b], first_basis[b], second_basis[b], start, held) for b in range(blocks)
+    ]
+    basis_new = jnp.stack([own for own, _ in refreshed])
+    complete_basis = jnp.stack([whole for _, whole in refreshed])
     moment_one = beta_one * moment_in + (1.0 - beta_one) * gradient.astype(jnp.float32)
     moment_half = moment_one.astype(jnp.bfloat16)
     gradient_block_list = gradient.reshape(blocks, order, width)
@@ -215,7 +305,7 @@
     unscaled_update = jnp.einsum(
         "rfu,rup->rfp", complete_basis, step_ratio, preferred_element_type=jnp.float32
     )
-    total = lax.psum(jnp.sum(unscaled_update * unscaled_update), ("owner", "fsdp"))
+    total = sum_everywhere(jnp.sum(unscaled_update * unscaled_update))
     count = gradient.shape[0] * lax.axis_size("owner") * width * lax.axis_size("fsdp")
     scale = jnp.sqrt(jnp.float32(count)) / (jnp.sqrt(total) + norm_eps)
     update = (unscaled_update * scale).reshape(blocks * order, width).astype(jnp.bfloat16)

time: 614 us -> 529 us (0.86); the launches traced: 610 us -> 519 us
  Pallas kernels: 152 us -> 101 us
  waiting for transfers between devices: 244 us -> 194 us
  matrix products: 144 us -> 186 us
  blocking collectives: 38.8 us -> 0 us
  local copies, waits for them, and re-layouts: 0.03 us -> 7.57 us
    pallas_call x1 -> x2, Pallas kernels: 152 us -> 90.4 us  [inverse_of_factor(): pl.pallas_call(functools.partial(factor_kernel, order // TILE), out_shape...]
    dot_general x4 -> x26, matrix products: 62.5 us -> 120 us  [dot(): lax.dot_general(left, right, (((1,), (across,)), ((), ())), preferred_ele...]
    all_gather x2 -> x3, waiting for transfers between devices: 243 us -> 192 us  [the longest x1 125 us: on_device(): factor = lax.all_gather(precond, 'fsdp', axis=1, tiled=True)]
    psum x1 -> x0, blocking collectives: 38.8 us -> none  [on_device(): lax.psum(jnp.sum(unscaled_update * unscaled_update), ('owner', 'fsdp'))]
    dot_general x1, matrix products: 33.8 us -> 15.7 us  [on_device(): jnp.einsum('rfu,rup->rfp', complete_basis, step_ratio, preferred_element_...]
    pallas_call x0 -> x1, Pallas kernels: none -> 10.8 us  [sum_everywhere(): pl.pallas_call(functools.partial(sum_kernel, owners, shards), out_shape=j...]
    dot_general x2 -> x4, matrix products: 31.1 us -> 33.7 us  [the longest x1 18.6 us: on_device(): jnp.einsum('aos,aol->asl', complete_basis, moment_block_list, preferred_e...]
  transfers between devices with their start and end apart: 2 -> 3, of which waited for: 2 -> 3; matrix products, arithmetic and copies ran while one was open for 2% -> 7% of each run, Pallas kernels for 0% -> 9%
where the time goes in v2:
time: 529 us; the launch traced here: 519 us
  waiting for transfers between devices  194 us (37%)
  matrix products  186 us (35%)
  Pallas kernels  101 us (19%)
  between operations  15.2 us (3%)
  other arithmetic  15.1 us (3%)
  local copies, waits for them, and re-layouts  7.57 us (1%)
    all_gather x1, waiting for transfers between devices, on_device(): factor = lax.all_gather(precond, 'fsdp', axis=1, tiled=True)  125 us
    dot_general x26, matrix products, dot(): lax.dot_general(left, right, (((1,), (across,)), ((), ())), preferred_ele...  120 us
    pallas_call x2, Pallas kernels, inverse_of_factor(): pl.pallas_call(functools.partial(factor_kernel, order // TILE), out_shape...  90.4 us
    all_gather x1, waiting for transfers between devices, on_device(): lax.all_gather(basis_old[:, :, :half], 'fsdp', axis=1, tiled=True)  65.6 us
    dot_general x1, matrix products, on_device(): jnp.einsum('aos,aol->asl', complete_basis, moment_block_list, preferred_e...  18.6 us
    dot_general x1, matrix products, on_device(): jnp.einsum('aos,aol->asl', complete_basis, gradient_block_list, preferred...  17 us
    dot_general x1, matrix products, on_device(): jnp.einsum('rfu,rup->rfp', complete_basis, step_ratio, preferred_element_...  15.7 us
    dot_general x3, matrix products, gram_of(): lax.dot_general(left, right, (((0,), (0,)), ((), ())), preferred_element_...  15.1 us
  transfers between devices with their start and end apart: 3, of which 3 were waited for; matrix products, arithmetic and copies ran while one was open for 7% of the time, Pallas kernels for 9%

profile of v2, /device:TPU:0, one launch (start us, length us, event | category | flops | bytes accessed | tf_op | source)
XLA Modules:
  0.0 518.9 jit_solution(13078806948366026296)
XLA Ops:
  7.2 2.2 fusion.65
  9.5 0.7 all-gather.4.cloned.1.call-update
  10.3 0.7 all-gather.8.cloned.1.call-update
  11.0 10.3 %multiply_add_fusion.1 = f32[2048,1024]{1,0:T(8,128)} fusion(bf16[2048,1024]{1,0:T(8,128)(2,1)} %param.7, f32[2048,1024]{1,0:T(8,128)} %param.8), kind=kLoop, calls=%fused_computation.9 | loop fusion | flops 8388608 | bytes 20971520 | tf_op jit(solution)/shard_map/add | solution.py:291
  21.2 65.6 %all-gather.6.cloned.1.call-done = bf16[1,2048,1024]{2,1,0:T(8,128)(2,1)} async-done(((bf16[1,256,1024]{2,1,0:T(8,128)(2,1)}), bf16[1,2048,1024]{2,1,0:T(8,128)(2,1)}) %all-gather.6.cloned.1.call-update) | async-done | bytes 4194320 | tf_op jit(solution)/shard_map/all_gather | solution.py:284
  86.8 125.4 %all-gather.4.cloned.1.call-done = bf16[1,2048,2048]{2,1,0:T(8,128)(2,1)} async-done(((bf16[1,256,2048]{2,1,0:T(8,128)(2,1)}), bf16[1,2048,2048]{2,1,0:T(8,128)(2,1)}) %all-gather.4.cloned.1.call-update) | async-done | bytes 8388624 | tf_op jit(solution)/shard_map/all_gather | solution.py:283
  212.2 12.5 %fusion.13 = bf16[2048,1024]{1,0:T(8,128)(2,1)S(1)} fusion(bf16[1,2048,1024]{2,1,0:T(8,128)(2,1)} %all-gather.6.cloned.1.call-done, bf16[1,2048,2048]{2,1,0:T(8,128)(2,1)} %all-gather.4.cloned.1.call-done), kind=kOutput, calls=%fused_computation.25 | convolution fusion | flops 8592031744 | bytes 16777216 | tf_op jit(solution)/shard_map/dot_general | solution.py:23
  224.7 4.6 fusion.68.gram_ref
  229.2 45.2 %shard_map.84 = (bf16[1024,1024]{1,0:T(8,128)(2,1)S(1)}, bf16[1024,1024]{1,0:T(8,128)(2,1)S(1)}) custom-call(f32[1024,1024]{1,0:T(8,128)S(1)} %fusion.68.gram_ref), custom_call_target="tpu_custom_call" | custom-call | flops 64424509440 | bytes 8388608 | tf_op jit(solution)/shard_map/pallas_call | solution.py:159
  274.4 4.6 fusion.69
  279.0 6.2 %add_convert_fusion.1 = bf16[2048,1024]{1,0:T(8,128)(2,1)} fusion(f32[2048,1024]{1,0:T(8,128)S(1)} %fusion.69, bf16[2048,1024]{1,0:T(8,128)(2,1)S(1)} %fusion.13, bf16[1024,1024]{1,0:T(8,128)(2,1)S(1)} %get-tuple-element.17), kind=kOutput, calls=%fused_computation.11 | convolution fusion | flops 4299161600 | bytes 18874368 | tf_op jit(solution)/shard_map/dot_general | solution.py:23
  285.2 1.4 all-gather.8.cloned.1.call-done
  286.6 12.9 %fusion.18 = bf16[1024,2048]{1,0:T(8,128)(2,1)S(1)} fusion(bf16[2048,1024]{1,0:T(8,128)(2,1)} %bitcast.50, bf16[1,2048,2048]{2,1,0:T(8,128)(2,1)} %all-gather.4.cloned.1.call-done), kind=kOutput, calls=%fused_computation.26 | convolution fusion | flops 8592031744 | bytes 16777216 | tf_op jit(solution)/shard_map/dot_general | solution.py:23
  299.6 2.0 copy-done.11
  301.6 4.5 fusion.71
  306.1 2.4 fusion.21
  308.4 2.4 fusion.53
  310.8 2.4 add_add_fusion.1
  313.2 2.3 fusion.55
  315.5 4.5 fusion.59
  320.0 2.4 fusion.56
  322.4 4.3 fusion.57
  326.7 6.1 %fusion.70 = f32[1024,1024]{1,0:T(8,128)} fusion(bf16[1024,2048]{1,0:T(8,128)(2,1)S(1)} %copy-done.12), kind=kOutput, calls=%fused_computation.77 | convolution fusion | flops 4294967296 | bytes 8388608 | tf_op jit(solution)/shard_map/dot_general | solution.py:185
  332.8 5.9 %add_subtract_fusion.gram_ref = f32[1024,1024]{1,0:T(8,128)S(1)} fusion(f32[1024,1024]{1,0:T(8,128)} %fusion.70, f32[1024,1024]{1,0:T(8,128)} %fusion.57, f32[1024,1024]{1,0:T(8,128)S(1)} %fusion.56, f32[1024,1024]{1,0:T(8,128)S(1)} %add_add_fusion.1), kind=kOutput, calls=%fused_computation.21 | convolution fusion | flops 2151677952 | bytes 20971520 | tf_op jit(solution)/shard_map/dot_general | solution.py:23
  338.7 45.2 %shard_map.85 = (bf16[1024,1024]{1,0:T(8,128)(2,1)S(1)}, bf16[1024,1024]{1,0:T(8,128)(2,1)S(1)}) custom-call(f32[1024,1024]{1,0:T(8,128)S(1)} %add_subtract_fusion.gram_ref), custom_call_target="tpu_custom_call" | custom-call | flops 64424509440 | bytes 8388608 | tf_op jit(solution)/shard_map/pallas_call | solution.py:159
  383.9 2.3 fusion.31
  386.2 2.9 fusion.25
  389.1 2.5 add_add_fusion
  391.6 2.4 fusion.48
  394.0 2.4 fusion.22
  396.4 2.4 add_negate_fusion
  398.8 0.8 fusion.28
  399.5 6.8 %fusion.44 = f32[2048,1024]{1,0:T(8,128)} fusion(bf16[2048,1024]{1,0:T(8,128)(2,1)S(1)} %copy-done.10, f32[1024,1024]{1,0:T(8,128)S(1)} %add_negate_fusion), kind=kOutput, calls=%fused_computation.53 | convolution fusion | flops 4296015872 | bytes 16777216 | tf_op jit(solution)/shard_map/dot_general | solution.py:23
  406.4 7.1 %fusion.46 = f32[2048,1024]{1,0:T(8,128)} fusion(bf16[2048,1024]{1,0:T(8,128)(2,1)S(1)} %copy-done.10, f32[1024,1024]{1,0:T(8,128)S(1)} %add_negate_fusion), kind=kOutput, calls=%fused_computation.55 | convolution fusion | flops 4299161600 | bytes 16777216 | tf_op jit(solution)/shard_map/dot_general | solution.py:23
  413.5 7.0 %fusion.72 = f32[2048,1024]{1,0:T(8,128)} fusion(bf16[1024,2048]{1,0:T(8,128)(2,1)S(1)} %copy-done.13, bf16[1024,1024]{1,0:T(8,128)(2,1)S(1)} %get-tuple-element.19), kind=kOutput, calls=%fused_computation.79 | convolution fusion | flops 4294967296 | bytes 14680064 | tf_op jit(solution)/shard_map/dot_general | solution.py:23
  420.4 1.8 convolution_add_fusion.1
  422.2 1.7 convolution_add_fusion.2
  424.0 14.5 %add_convert_fusion = bf16[2048,1024]{1,0:T(8,128)(2,1)} fusion(f32[2048,1024]{1,0:T(8,128)} %fusion.72, f32[2048,1024]{1,0:T(8,128)} %fusion.46, f32[2048,1024]{1,0:T(8,128)} %fusion.44, bf16[1024,2048]{1,0:T(8,128)(2,1)} %copy-done.11, bf16[1024,1024]{1,0:T(8,128)(2,1)S(1)} %get-tuple-element.18), kind=kOutput, calls=%fused_computation.10 | convolution fusion | flops 4303355904 | bytes 35651584 | tf_op jit(solution)/shard_map/dot_general | solution.py:23
  438.4 17.0 %multiply_add_fusion = f32[2048,1024]{1,0:T(8,128)} fusion(f32[2048,1024]{1,0:T(8,128)} %param.9, bf16[2048,1024]{1,0:T(8,128)(2,1)S(1)} %copy-done.6, bf16[2048,1024]{1,0:T(8,128)(2,1)} %add_convert_fusion, bf16[2048,1024]{1,0:T(8,128)(2,1)} %add_convert_fusion.1), kind=kOutput, calls=%fused_computation.8 | convolution fusion | flops 8615100416 | bytes 29360128 | tf_op jit(solution)/shard_map/aos,aol->asl/dot_general | solution.py:295
  455.4 18.6 %divide_convert_fusion.1.clone.5 = bf16[2048,1024]{1,0:T(8,128)(2,1)} fusion(f32[2048,1024]{1,0:T(8,128)} %multiply_add_fusion, f32[2048,1024]{1,0:T(8,128)} %multiply_add_fusion.1, bf16[2048,1024]{1,0:T(8,128)(2,1)} %add_convert_fusion, bf16[2048,1024]{1,0:T(8,128)(2,1)} %add_convert_fusion.1), kind=kOutput, calls=%fused_computation.7.clone.clone.clone.clone.2 | convolution fusion | flops 8615100416 | bytes 29360128 | tf_op jit(solution)/shard_map/aos,aol->asl/dot_general | solution.py:298
  474.0 15.7 %multiply_reduce_fusion = (f32[]{:T(128)}, f32[2048,1024]{1,0:T(8,128)}) fusion(bf16[2048,1024]{1,0:T(8,128)(2,1)S(1)} %copy-done.14, bf16[2048,1024]{1,0:T(8,128)(2,1)} %add_convert_fusion.1, bf16[2048,1024]{1,0:T(8,128)(2,1)} %divide_convert_fusion.1.clone.5), kind=kOutput, calls=%fused_computation.6 | convolution fusion | flops 8610906112 | bytes 20971524 | tf_op jit(solution)/shard_map/rfu,rup->rfp/dot_general | solution.py:305
  489.7 1.2 broadcast_in_dim.3.value_ref
  490.9 10.8 %shard_map.86 = f32[8,128]{1,0:T(8,128)} custom-call(f32[8,128]{1,0:T(8,128)} %broadcast_in_dim.3.value_ref), custom_call_target="tpu_custom_call" | custom-call | tf_op jit(solution)/shard_map/pallas_call | solution.py:259
  501.8 1.3 slice.11
  503.7 2.6 fusion.23
  506.4 1.5 maximum_bitcast_fusion
  507.9 0.8 copy-done.5
  508.6 3.3 multiply_convert_fusion
  (32 shorter events, 0.2 us)
Async XLA Ops:
  7.2 79.7 %all-gather.6.cloned.1.call-start = ((), (), s32[]{:S(2)}) async-start(), calls=%async_computation.1 | async-start | bytes 4718592 | tf_op jit(solution)/shard_map/all_gather | solution.py:284
  9.5 202.7 %all-gather.4.cloned.1.call-start = ((), (), s32[]{:S(2)}) async-start(), calls=%async_computation | async-start | bytes 9437184 | tf_op jit(solution)/shard_map/all_gather | solution.py:283
  10.2 276.4 %all-gather.8.cloned.1.call-start = ((), (), s32[]{:S(2)}) async-start(), calls=%async_computation.2 | async-start | bytes 4718592 | tf_op jit(solution)/shard_map/all_gather | solution.py:285
  224.7 54.3 %copy-start.8 = (bf16[2048,1024]{1,0:T(8,128)(2,1)}, bf16[2048,1024]{1,0:T(8,128)(2,1)S(1)}, u32[]{:S(2)}) copy-start(bf16[2048,1024]{1,0:T(8,128)(2,1)S(1)} %fusion.13) | copy-start | bytes 12582916
  274.4 4.6 copy-start.2
  286.6 14.9 %copy-start.9 = (bf16[2048,1024]{1,0:T(8,128)(2,1)S(1)}, bf16[2048,1024]{1,0:T(8,128)(2,1)}, u32[]{:S(2)}) copy-start(bf16[2048,1024]{1,0:T(8,128)(2,1)} %copy-done.8) | copy-start | bytes 12582916
  299.5 2.0 copy-start.11
  306.0 2.4 copy-start.3
  322.4 4.3 copy-start.12
  383.9 40.0 %copy-start = (bf16[1024,1024]{1,0:T(8,128)(2,1)}, bf16[1024,1024]{1,0:T(8,128)(2,1)S(1)}, u32[]{:S(2)}) copy-start(bf16[1024,1024]{1,0:T(8,128)(2,1)S(1)} %get-tuple-element.18) | copy-start | bytes 6291460
  383.9 5.2 %copy-start.4 = (f32[1024,1024]{1,0:T(8,128)S(1)}, f32[1024,1024]{1,0:T(8,128)}, u32[]{:S(2)}) copy-start(f32[1024,1024]{1,0:T(8,128)} %fusion.59) | copy-start | bytes 12582916
  396.3 2.4 copy-start.10
  406.4 7.1 %copy-start.13 = (bf16[1024,2048]{1,0:T(8,128)(2,1)S(1)}, bf16[1024,2048]{1,0:T(8,128)(2,1)}, u32[]{:S(2)}) copy-start(bf16[1024,2048]{1,0:T(8,128)(2,1)} %copy-done.11) | copy-start | bytes 12582916
  424.0 14.5 %copy-start.6 = (bf16[2048,1024]{1,0:T(8,128)(2,1)S(1)}, bf16[2048,1024]{1,0:T(8,128)(2,1)}, u32[]{:S(2)}) copy-start(bf16[2048,1024]{1,0:T(8,128)(2,1)} %param.7) | copy-start | bytes 12582916
  455.4 18.6 %copy-start.14 = (bf16[2048,1024]{1,0:T(8,128)(2,1)S(1)}, bf16[2048,1024]{1,0:T(8,128)(2,1)}, u32[]{:S(2)}) copy-start(bf16[2048,1024]{1,0:T(8,128)(2,1)} %add_convert_fusion) | copy-start | bytes 12582916
  474.0 29.7 %copy-start.1 = (bf16[1024,1024]{1,0:T(8,128)(2,1)S(1)}, bf16[1024,1024]{1,0:T(8,128)(2,1)}, u32[]{:S(2)}) copy-start(bf16[1024,1024]{1,0:T(8,128)(2,1)} %copy-done) | copy-start | bytes 6291460
  489.7 16.7 %copy-start.7 = (f32[256,1024]{1,0:T(8,128)S(1)}, f32[256,1024]{1,0:T(8,128)}, u32[]{:S(2)}) copy-start(f32[256,1024]{1,0:T(8,128)} %convolution_add_fusion.2) | copy-start | bytes 3145732
  503.7 4.9 copy-start.5
Sparse Core Ops, SparseCore 0:
  10.7 76.0 all-gather.5
  89.0 123.1 all-gather.3
  214.9 71.7 all-gather.7

commit v3 on v2

--- a/solution.py
+++ b/solution.py
@@ -200,14 +200,41 @@
     inverse_second = inverse_of_factor(corner)
     inverse_side = split(-dot3(inverse_second, split(dot3(side, inverse_first, 0)), 0))
 
-    def second_columns(first_rows, second_rows):
-        return rotate(first_rows, inverse_side) + rotate(second_rows, inverse_second)
-
-    basis_second = second_columns(power_first, power_second).astype(jnp.bfloat16)
-    own_first = lax.dynamic_slice_in_dim(power_first, start, count, 0)
-    own_second = lax.dynamic_slice_in_dim(power_second, start, count, 0)
-    own = [rotate(own_first, inverse_first), second_columns(own_first, own_second)]
+    second = [
+        jnp.concatenate(pair, axis=1) for pair in zip(inverse_side, inverse_second, strict=True)
+    ]
+    power = jnp.concatenate([power_first, power_second], axis=1)
+    basis_second = rotate(power, second).astype(jnp.bfloat16)
+    own_power = lax.dynamic_slice_in_dim(power, start, count, 0)
+    own = [rotate(own_power[:, : power_first.shape[1]], inverse_first), rotate(own_power, second)]
     return jnp.concatenate(own, axis=1), jnp.concatenate([basis_first, basis_second], axis=1)
+
+
+def symmetric_kernel(shards, sent_ref, whole_ref):
+    held = whole_ref.shape[0] // shards
+
+    def part(index):
+        return pl.ds(pl.multiple_of(index * held, held), held)
+
+    @pl.loop(0, shards)
+    def _(i):
+        for ahead in range(shards // 2 + 1):
+            other = lax.rem(i + ahead, shards)
+            block = sent_ref[part(i), ahead * held : (ahead + 1) * held]
+            whole_ref[part(i), part(other)] = block
+            if 0 < 2 * ahead < shards:
+                whole_ref[part(other), part(i)] = block.T
+
+
+def symmetric_whole(sent, shards):
+    order = sent.shape[0]
+    return pl.pallas_call(
+        functools.partial(symmetric_kernel, shards),
+        out_shape=jax.ShapeDtypeStruct((order, order), sent.dtype),
+        in_specs=[pl.BlockSpec(memory_space=pltpu.VMEM)],
+        out_specs=pl.BlockSpec(memory_space=pltpu.VMEM),
+        compiler_params=pltpu.CompilerParams(vmem_limit_bytes=40 * 1024 * 1024),
+    )(sent)
 
 
 def sum_kernel(
@@ -280,8 +307,16 @@
     width = gradient.shape[1]
     half = order // 2
     start = lax.axis_index("fsdp") * held
-    factor = lax.all_gather(precond, "fsdp", axis=1, tiled=True)
-    first_basis = lax.all_gather(basis_old[:, :, :half], "fsdp", axis=1, tiled=True)
+    shards = lax.axis_size("fsdp")
+    sent = held * (shards // 2 + 1)
+    ahead = lax.dynamic_slice_in_dim(
+        jnp.concatenate([precond, precond[:, :, :sent]], axis=2), start, sent, 2
+    )
+    gathered = lax.all_gather(
+        jnp.concatenate([ahead, basis_old[:, :, :half]], axis=2), "fsdp", axis=1, tiled=True
+    )
+    factor = [symmetric_whole(gathered[b], shards) for b in range(blocks)]
+    first_basis = gathered[:, :, sent:]
     second_basis = lax.all_gather(basis_old[:, :, half:], "fsdp", axis=1, tiled=True)
     refreshed = [
         refresh(factor[b], first_basis[b], second_basis[b], start, held) for b in range(blocks)

time: 529 us -> 474 us (0.90)
  waiting for transfers between devices: 194 us -> 130 us
  other arithmetic: 15.1 us -> 21.1 us
    all_gather x2 -> x1, waiting for transfers between devices: 191 us -> 130 us  [on_device(): lax.all_gather(jnp.concatenate([ahead, basis_old[:, :, :half]], axis=2),...]
    pallas_call x0 -> x1, Pallas kernels: none -> 5.37 us  [symmetric_whole(): pl.pallas_call(functools.partial(symmetric_kernel, shards), out_shape=jax...]
    dot_general x26 -> x22, matrix products: 120 us -> 117 us  [dot(): lax.dot_general(left, right, (((1,), (across,)), ((), ())), preferred_ele...]
  transfers between devices with their start and end apart: 3 -> 2, of which waited for: 3 -> 1; matrix products, arithmetic and copies ran while one was open for 7% -> 8% of each run, Pallas kernels for 9% -> 11%
where the time goes in v3:
time: 474 us; the launch traced here: 466 us
  matrix products  183 us (39%)
  waiting for transfers between devices  130 us (27%)
  Pallas kernels  106 us (22%)
  other arithmetic  21.1 us (4%)
  between operations  15.5 us (3%)
  local copies, waits for them, and re-layouts  9.84 us (2%)
    all_gather x1, waiting for transfers between devices, on_device(): lax.all_gather(jnp.concatenate([ahead, basis_old[:, :, :half]], axis=2),...  130 us
    dot_general x22, matrix products, dot(): lax.dot_general(left, right, (((1,), (across,)), ((), ())), preferred_ele...  117 us
    pallas_call x2, Pallas kernels, inverse_of_factor(): pl.pallas_call(functools.partial(factor_kernel, order // TILE), out_shape...  90.3 us
    dot_general x1, matrix products, on_device(): jnp.einsum('aos,aol->asl', complete_basis, moment_block_list, preferred_e...  18.6 us
    dot_general x1, matrix products, on_device(): jnp.einsum('aos,aol->asl', complete_basis, gradient_block_list, preferred...  17 us
    dot_general x1, matrix products, on_device(): jnp.einsum('rfu,rup->rfp', complete_basis, step_ratio, preferred_element_...  15.1 us
    dot_general x3, matrix products, gram_of(): lax.dot_general(left, right, (((0,), (0,)), ((), ())), preferred_element_...  15.1 us
    pallas_call x1, Pallas kernels, sum_everywhere(): pl.pallas_call(functools.partial(sum_kernel, owners, shards), out_shape=j...  10.8 us
  transfers between devices with their start and end apart: 2, of which 1 were waited for; matrix products, arithmetic and copies ran while one was open for 8% of the time, Pallas kernels for 11%

profile of v3, /device:TPU:0, one launch (start us, length us, event | category | flops | bytes accessed | tf_op | source)
XLA Modules:
  0.0 465.9 jit_solution(8820008889152815771)
XLA Ops:
  7.2 1.1 slice.18
  8.3 2.1 fusion.48
  10.4 1.3 fusion.18
  11.7 1.1 pad_maximum_fusion.17
  12.9 0.0 all-gather.5.cloned.1.call-start
  12.9 0.7 all-gather.5.cloned.1.call-update
  13.6 10.4 %multiply_add_fusion.1 = f32[2048,1024]{1,0:T(8,128)} fusion(bf16[2048,1024]{1,0:T(8,128)(2,1)} %param.7, f32[2048,1024]{1,0:T(8,128)} %param.8), kind=kLoop, calls=%fused_computation.8 | loop fusion | flops 8388608 | bytes 20971520 | tf_op jit(solution)/shard_map/add | solution.py:326
  24.0 129.6 %all-gather.3.cloned.1.call-done = bf16[1,2048,2304]{2,1,0:T(8,128)(2,1)} async-done(((bf16[1,256,2304]{2,1,0:T(8,128)(2,1)}), bf16[1,2048,2304]{2,1,0:T(8,128)(2,1)}) %all-gather.3.cloned.1.call-update) | async-done | bytes 9437200 | tf_op jit(solution)/shard_map/all_gather | solution.py:315
  153.6 5.4 %shard_map.84 = bf16[2048,2048]{1,0:T(8,128)(2,1)S(1)} custom-call(bf16[2048,2304]{1,0:T(8,128)(2,1)} %bitcast.38), custom_call_target="tpu_custom_call" | custom-call | tf_op jit(solution)/shard_map/pallas_call | solution.py:231
  159.0 13.0 %fusion.11 = bf16[2048,1024]{0,1:T(8,128)(2,1)S(1)} fusion(bf16[2048,2048]{1,0:T(8,128)(2,1)S(1)} %shard_map.84, bf16[1,2048,2304]{2,1,0:T(8,128)(2,1)} %all-gather.3.cloned.1.call-done), kind=kOutput, calls=%fused_computation.29 | convolution fusion | flops 8592031744 | bytes 16777216 | tf_op jit(solution)/shard_map/dot_general | solution.py:23
  172.0 1.9 copy-done.4
  173.9 4.5 fusion.51.gram_ref
  178.5 45.1 %shard_map.85 = (bf16[1024,1024]{1,0:T(8,128)(2,1)S(1)}, bf16[1024,1024]{1,0:T(8,128)(2,1)S(1)}) custom-call(f32[1024,1024]{1,0:T(8,128)S(1)} %fusion.51.gram_ref), custom_call_target="tpu_custom_call" | custom-call | flops 64424509440 | bytes 8388608 | tf_op jit(solution)/shard_map/pallas_call | solution.py:159
  223.6 4.6 fusion.52
  228.2 6.3 %add_convert_fusion.1 = bf16[2048,1024]{1,0:T(8,128)(2,1)} fusion(f32[2048,1024]{1,0:T(8,128)S(1)} %fusion.52, bf16[2048,1024]{0,1:T(8,128)(2,1)S(1)} %copy-done.5, bf16[1024,1024]{1,0:T(8,128)(2,1)S(1)} %get-tuple-element.17), kind=kOutput, calls=%fused_computation.10 | convolution fusion | flops 4299161600 | bytes 18874368 | tf_op jit(solution)/shard_map/dot_general | solution.py:23
  234.5 21.5 %convolution_convert_fusion = bf16[2048,1024]{0,1:T(8,128)(2,1)S(1)} fusion(bf16[2048,2048]{1,0:T(8,128)(2,1)} %copy-done, bf16[2048,1024]{1,0:T(8,128)(2,1)} %bitcast.39), kind=kOutput, calls=%fused_computation.30 | convolution fusion | flops 8592031744 | bytes 16777216 | tf_op jit(solution)/shard_map/dot_general | solution.py:23
  256.0 4.5 fusion.54
  260.5 2.4 fusion.14
  262.9 2.4 fusion.36
  265.3 2.4 add_add_fusion.1
  267.7 2.3 fusion.38
  270.1 2.6 fusion.42
  272.6 2.4 fusion.39
  275.0 4.4 fusion.40
  279.4 6.1 %fusion.53 = f32[1024,1024]{1,0:T(8,128)} fusion(bf16[2048,1024]{0,1:T(8,128)(2,1)S(1)} %copy-done.9), kind=kOutput, calls=%fused_computation.74 | convolution fusion | flops 4294967296 | bytes 8388608 | tf_op jit(solution)/shard_map/dot_general | solution.py:185
  285.4 0.1 fusion.17
  285.6 1.8 fusion.20
  287.4 5.9 %add_subtract_fusion.gram_ref = f32[1024,1024]{1,0:T(8,128)S(1)} fusion(f32[1024,1024]{1,0:T(8,128)} %fusion.53, f32[1024,1024]{1,0:T(8,128)} %fusion.40, f32[1024,1024]{1,0:T(8,128)S(1)} %fusion.39, f32[1024,1024]{1,0:T(8,128)S(1)} %add_add_fusion.1), kind=kOutput, calls=%fused_computation.25 | convolution fusion | flops 2151677952 | bytes 20971520 | tf_op jit(solution)/shard_map/dot_general | solution.py:23
  293.3 45.2 %shard_map.86 = (bf16[1024,1024]{1,0:T(8,128)(2,1)S(1)}, bf16[1024,1024]{1,0:T(8,128)(2,1)S(1)}) custom-call(f32[1024,1024]{1,0:T(8,128)S(1)} %add_subtract_fusion.gram_ref), custom_call_target="tpu_custom_call" | custom-call | flops 64424509440 | bytes 8388608 | tf_op jit(solution)/shard_map/pallas_call | solution.py:159
  338.6 2.3 add_add_fusion
  340.9 2.4 fusion.31
  343.3 2.4 fusion.15
  345.6 4.0 subtract_convert_fusion
  349.6 1.4 copy-done.14
  351.0 1.3 fusion.12
  352.3 0.8 copy-done.7
  353.2 13.7 %fusion = f32[2048,1024]{1,0:T(8,128)} fusion(bf16[2048,1024]{0,1:T(8,128)(2,1)} %copy-done.8, bf16[2048,1024]{0,1:T(8,128)(2,1)S(1)} %copy-done.7, bf16[1024,1024]{1,0:T(8,128)(2,1)S(1)} %get-tuple-element.18, bf16[1024,1024]{1,0:T(8,128)(2,1)} %copy-done.14), kind=kOutput, calls=%fused_computation.11 | convolution fusion | flops 8615100416 | bytes 20971520 | tf_op jit(solution)/shard_map/dot_general | solution.py:23
  366.9 1.8 convolution_add_fusion
  368.6 2.4 fusion.16
  371.0 14.7 %add_convert_fusion = bf16[2048,1024]{1,0:T(8,128)(2,1)} fusion(f32[2048,1024]{1,0:T(8,128)} %fusion, bf16[2048,1024]{0,1:T(8,128)(2,1)} %copy-done.8, bf16[2048,1024]{0,1:T(8,128)(2,1)} %copy-done.4, bf16[1024,1024]{1,0:T(8,128)(2,1)S(1)} %get-tuple-element.19, bf16[1024,1024]{1,0:T(8,128)(2,1)} %get-tuple-element.20), kind=kOutput, calls=%fused_computation.9 | convolution fusion | flops 8619294720 | bytes 25165824 | tf_op jit(solution)/shard_map/dot_general | solution.py:23
  385.8 17.0 %multiply_add_fusion = f32[2048,1024]{1,0:T(8,128)} fusion(f32[2048,1024]{1,0:T(8,128)} %param.9, bf16[2048,1024]{1,0:T(8,128)(2,1)S(1)} %copy-done.3, bf16[2048,1024]{1,0:T(8,128)(2,1)} %add_convert_fusion, bf16[2048,1024]{1,0:T(8,128)(2,1)} %add_convert_fusion.1), kind=kOutput, calls=%fused_computation.7 | convolution fusion | flops 8615100416 | bytes 29360128 | tf_op jit(solution)/shard_map/aos,aol->asl/dot_general | solution.py:330
  402.7 18.6 %divide_convert_fusion.1.clone.5 = bf16[2048,1024]{1,0:T(8,128)(2,1)} fusion(f32[2048,1024]{1,0:T(8,128)} %multiply_add_fusion, f32[2048,1024]{1,0:T(8,128)} %multiply_add_fusion.1, bf16[2048,1024]{1,0:T(8,128)(2,1)} %add_convert_fusion, bf16[2048,1024]{1,0:T(8,128)(2,1)} %add_convert_fusion.1), kind=kOutput, calls=%fused_computation.6.clone.clone.clone.clone.2 | convolution fusion | flops 8615100416 | bytes 29360128 | tf_op jit(solution)/shard_map/aos,aol->asl/dot_general | solution.py:333
  421.3 15.1 %multiply_reduce_fusion = (f32[]{:T(128)}, f32[2048,1024]{1,0:T(8,128)}) fusion(bf16[2048,1024]{1,0:T(8,128)(2,1)} %add_convert_fusion, bf16[2048,1024]{1,0:T(8,128)(2,1)S(1)} %copy-done.15, bf16[2048,1024]{1,0:T(8,128)(2,1)} %divide_convert_fusion.1.clone.5), kind=kOutput, calls=%fused_computation.5 | convolution fusion | flops 8610906112 | bytes 20971524 | tf_op jit(solution)/shard_map/rfu,rup->rfp/dot_general | solution.py:340
  436.5 1.2 broadcast_in_dim.3.value_ref
  437.7 10.8 %shard_map.87 = f32[8,128]{1,0:T(8,128)} custom-call(f32[8,128]{1,0:T(8,128)} %broadcast_in_dim.3.value_ref), custom_call_target="tpu_custom_call" | custom-call | tf_op jit(solution)/shard_map/pallas_call | solution.py:286
  448.5 1.2 slice.22
  450.4 1.5 maximum_bitcast_fusion
  451.9 6.7 %multiply_convert_fusion = bf16[2048,1024]{1,0:T(8,128)(2,1)} fusion(f32[2048,1024]{1,0:T(8,128)} %get-tuple-element.26, f32[]{:T(128)} %bitcast.3), kind=kLoop, calls=%fused_computation.4 | loop fusion | flops 4194304 | bytes 12582916 | tf_op jit(solution)/shard_map/convert_element_type | solution.py:346
  (32 shorter events, 0.1 us)
Async XLA Ops:
  7.2 146.5 %all-gather.3.cloned.1.call-start = ((), (), s32[]{:S(2)}) async-start(), calls=%async_computation | async-start | bytes 10616832 | tf_op jit(solution)/shard_map/all_gather | solution.py:315
  12.9 221.6 %all-gather.5.cloned.1.call-start = ((), (), s32[]{:S(2)}) async-start(), calls=%async_computation.1 | async-start | bytes 4718592 | tf_op jit(solution)/shard_map/all_gather | solution.py:320
  159.0 13.0 %copy-start = (bf16[2048,2048]{1,0:T(8,128)(2,1)}, bf16[2048,2048]{1,0:T(8,128)(2,1)S(1)}, u32[]{:S(2)}) copy-start(bf16[2048,2048]{1,0:T(8,128)(2,1)S(1)} %shard_map.84) | copy-start | bytes 25165828
  172.0 1.9 copy-start.4
  178.5 45.1 %copy-start.5 = (bf16[2048,1024]{0,1:T(8,128)(2,1)S(1)}, bf16[2048,1024]{0,1:T(8,128)(2,1)}, u32[]{:S(2)}) copy-start(bf16[2048,1024]{0,1:T(8,128)(2,1)} %copy-done.4) | copy-start | bytes 12582916
  223.6 4.6 copy-start.1
  234.5 21.5 %copy-start.6 = (bf16[2048,1024]{0,1:T(8,128)(2,1)S(1)}, bf16[2048,1024]{0,1:T(8,128)(2,1)}, u32[]{:S(2)}) copy-start(bf16[2048,1024]{0,1:T(8,128)(2,1)} %copy-done.4) | copy-start | bytes 12582916
  256.0 4.5 copy-start.8
  260.5 2.4 copy-start.2
  275.0 4.4 copy-start.9
  349.6 1.4 copy-start.14
  351.0 2.2 copy-start.7
  353.2 13.7 %copy-start.10 = (f32[256,1024]{1,0:T(8,128)S(1)}, f32[256,1024]{1,0:T(8,128)}, u32[]{:S(2)}) copy-start(f32[256,1024]{1,0:T(8,128)} %fusion.20) | copy-start | bytes 3145732
  366.8 1.8 copy-start.13
  371.0 14.7 %copy-start.3 = (bf16[2048,1024]{1,0:T(8,128)(2,1)S(1)}, bf16[2048,1024]{1,0:T(8,128)(2,1)}, u32[]{:S(2)}) copy-start(bf16[2048,1024]{1,0:T(8,128)(2,1)} %param.7) | copy-start | bytes 12582916
  402.7 18.6 %copy-start.15 = (bf16[2048,1024]{1,0:T(8,128)(2,1)S(1)}, bf16[2048,1024]{1,0:T(8,128)(2,1)}, u32[]{:S(2)}) copy-start(bf16[2048,1024]{1,0:T(8,128)(2,1)} %add_convert_fusion.1) | copy-start | bytes 12582916
  421.3 29.1 %copy-start.11 = (f32[256,1024]{1,0:T(8,128)S(1)}, f32[256,1024]{1,0:T(8,128)}, u32[]{:S(2)}) copy-start(f32[256,1024]{1,0:T(8,128)} %convolution_add_fusion) | copy-start | bytes 3145732
  421.3 29.1 %copy-start.12 = (f32[256,1024]{1,0:T(8,128)S(1)}, f32[256,1024]{1,0:T(8,128)}, u32[]{:S(2)}) copy-start(f32[256,1024]{1,0:T(8,128)} %fusion.16) | copy-start | bytes 3145732
Sparse Core Ops, SparseCore 0:
  13.0 140.5 all-gather.2
  156.3 71.5 all-gather.4

commit v4 on v3

--- a/solution.py
+++ b/solution.py
@@ -203,7 +203,7 @@
     second = [
         jnp.concatenate(pair, axis=1) for pair in zip(inverse_side, inverse_second, strict=True)
     ]
-    power = jnp.concatenate([power_first, power_second], axis=1)
+    power = lax.optimization_barrier(jnp.concatenate([power_first, power_second], axis=1))
     basis_second = rotate(power, second).astype(jnp.bfloat16)
     own_power = lax.dynamic_slice_in_dim(power, start, count, 0)
     own = [rotate(own_power[:, : power_first.shape[1]], inverse_first), rotate(own_power, second)]

time: 474 us -> 474 us (level)
  other arithmetic: 21.1 us -> 29.5 us
  matrix products: 183 us -> 176 us
    dot_general x22, matrix products: 117 us -> 107 us  [dot(): lax.dot_general(left, right, (((1,), (across,)), ((), ())), preferred_ele...]
    concatenate x1, other arithmetic: 0.14 us -> 8.53 us  [refresh(): jnp.concatenate([power_first, power_second], axis=1)]
where the time goes in v4:
time: 474 us; the launch traced here: 466 us
  matrix products  176 us (37%)
  waiting for transfers between devices  130 us (27%)
  Pallas kernels  106 us (22%)
  other arithmetic  29.5 us (6%)
  between operations  15.3 us (3%)
  local copies, waits for them, and re-layouts  7.86 us (2%)
    all_gather x1, waiting for transfers between devices, on_device(): lax.all_gather(jnp.concatenate([ahead, basis_old[:, :, :half]], axis=2),...  130 us
    dot_general x22, matrix products, dot(): lax.dot_general(left, right, (((1,), (across,)), ((), ())), preferred_ele...  107 us
    pallas_call x2, Pallas kernels, inverse_of_factor(): pl.pallas_call(functools.partial(factor_kernel, order // TILE), out_shape...  90 us
    dot_general x1, matrix products, on_device(): jnp.einsum('aos,aol->asl', complete_basis, moment_block_list, preferred_e...  18.6 us
    dot_general x3, matrix products, gram_of(): lax.dot_general(left, right, (((0,), (0,)), ((), ())), preferred_element_...  18.6 us
    dot_general x1, matrix products, on_device(): jnp.einsum('aos,aol->asl', complete_basis, gradient_block_list, preferred...  16.9 us
    dot_general x1, matrix products, on_device(): jnp.einsum('rfu,rup->rfp', complete_basis, step_ratio, preferred_element_...  15.1 us
    pallas_call x1, Pallas kernels, sum_everywhere(): pl.pallas_call(functools.partial(sum_kernel, owners, shards), out_shape=j...  10.8 us
  transfers between devices with their start and end apart: 2, of which 1 were waited for; matrix products, arithmetic and copies ran while one was open for 8% of the time, Pallas kernels for 11%

profile of v4, /device:TPU:0, one launch (start us, length us, event | category | flops | bytes accessed | tf_op | source)
XLA Modules:
  0.0 465.5 jit_solution(7661034797011630626)
XLA Ops:
  7.2 0.0 all-gather.3.cloned.1.call-start
  7.2 1.1 slice.18
  8.4 2.1 fusion.53
  10.4 1.3 fusion.18
  11.7 1.1 pad_maximum_fusion.13
  12.9 0.0 all-gather.5.cloned.1.call-start
  12.9 0.7 all-gather.5.cloned.1.call-update
  13.6 10.4 %multiply_add_fusion.1 = f32[2048,1024]{1,0:T(8,128)} fusion(bf16[2048,1024]{1,0:T(8,128)(2,1)} %param.7, f32[2048,1024]{1,0:T(8,128)} %param.8), kind=kLoop, calls=%fused_computation.6 | loop fusion | flops 8388608 | bytes 20971520 | tf_op jit(solution)/shard_map/add | solution.py:326
  24.0 129.6 %all-gather.3.cloned.1.call-done = bf16[1,2048,2304]{2,1,0:T(8,128)(2,1)} async-done(((bf16[1,256,2304]{2,1,0:T(8,128)(2,1)}), bf16[1,2048,2304]{2,1,0:T(8,128)(2,1)}) %all-gather.3.cloned.1.call-update) | async-done | bytes 9437200 | tf_op jit(solution)/shard_map/all_gather | solution.py:315
  153.6 5.4 %shard_map.84 = bf16[2048,2048]{1,0:T(8,128)(2,1)S(1)} custom-call(bf16[2048,2304]{1,0:T(8,128)(2,1)} %bitcast.40), custom_call_target="tpu_custom_call" | custom-call | tf_op jit(solution)/shard_map/pallas_call | solution.py:231
  159.0 13.0 %fusion.9 = bf16[2048,1024]{0,1:T(8,128)(2,1)S(1)} fusion(bf16[2048,2048]{1,0:T(8,128)(2,1)S(1)} %shard_map.84, bf16[1,2048,2304]{2,1,0:T(8,128)(2,1)} %all-gather.3.cloned.1.call-done), kind=kOutput, calls=%fused_computation.25 | convolution fusion | flops 8592031744 | bytes 16777216 | tf_op jit(solution)/shard_map/dot_general | solution.py:23
  172.0 2.0 copy-done.5
  174.0 4.5 fusion.56.gram_ref
  178.5 45.0 %shard_map.85 = (bf16[1024,1024]{1,0:T(8,128)(2,1)S(1)}, bf16[1024,1024]{1,0:T(8,128)(2,1)S(1)}) custom-call(f32[1024,1024]{1,0:T(8,128)S(1)} %fusion.56.gram_ref), custom_call_target="tpu_custom_call" | custom-call | flops 64424509440 | bytes 8388608 | tf_op jit(solution)/shard_map/pallas_call | solution.py:159
  223.5 4.6 fusion.57
  228.1 6.2 %add_convert_fusion.1 = bf16[2048,1024]{1,0:T(8,128)(2,1)} fusion(f32[2048,1024]{1,0:T(8,128)S(1)} %fusion.57, bf16[2048,1024]{0,1:T(8,128)(2,1)S(1)} %copy-done.6, bf16[1024,1024]{1,0:T(8,128)(2,1)S(1)} %get-tuple-element.17), kind=kOutput, calls=%fused_computation.8 | convolution fusion | flops 4299161600 | bytes 18874368 | tf_op jit(solution)/shard_map/dot_general | solution.py:23
  234.4 14.1 %convolution_convert_fusion = bf16[2048,1024]{0,1:T(8,128)(2,1)} fusion(bf16[2048,2048]{1,0:T(8,128)(2,1)} %copy-done, bf16[2048,1024]{1,0:T(8,128)(2,1)} %bitcast.41), kind=kOutput, calls=%fused_computation.26 | convolution fusion | flops 8592031744 | bytes 16777216 | tf_op jit(solution)/shard_map/dot_general | solution.py:23
  248.5 8.5 %pad_maximum_fusion = bf16[2048,2048]{0,1:T(8,128)(2,1)} fusion(bf16[2048,1024]{0,1:T(8,128)(2,1)} %convolution_convert_fusion, bf16[2048,1024]{0,1:T(8,128)(2,1)} %copy-done.5), kind=kLoop, calls=%fused_computation | loop fusion | flops 16777216 | bytes 16777216 | tf_op jit(solution)/shard_map/concatenate | solution.py:206
  257.0 8.0 %fusion.59 = f32[1024,1024]{1,0:T(8,128)S(1)} fusion(bf16[2048,1024]{0,1:T(8,128)(2,1)} %convolution_convert_fusion, bf16[2048,1024]{0,1:T(8,128)(2,1)} %copy-done.5), kind=kOutput, calls=%fused_computation.78 | convolution fusion | flops 4294967296 | bytes 12582912 | tf_op jit(solution)/shard_map/dot_general | solution.py:185
  265.0 2.4 fusion.13
  267.4 2.4 fusion.40
  269.8 2.4 add_add_fusion.1
  272.2 2.3 fusion.42
  274.6 4.3 fusion.46
  278.9 2.4 fusion.43
  281.3 2.6 fusion.44
  283.9 6.1 %fusion.58 = f32[1024,1024]{1,0:T(8,128)} fusion(bf16[2048,1024]{0,1:T(8,128)(2,1)S(1)} %copy-done.7), kind=kOutput, calls=%fused_computation.77 | convolution fusion | flops 4294967296 | bytes 8388608 | tf_op jit(solution)/shard_map/dot_general | solution.py:185
  290.0 1.8 fusion.20
  291.8 2.9 convolution_add_fusion
  294.6 4.7 %add_subtract_fusion.gram_ref = f32[1024,1024]{1,0:T(8,128)S(1)} fusion(f32[1024,1024]{1,0:T(8,128)} %fusion.58, f32[1024,1024]{1,0:T(8,128)S(1)} %fusion.44, f32[1024,1024]{1,0:T(8,128)S(1)} %fusion.43, f32[1024,1024]{1,0:T(8,128)S(1)} %add_add_fusion.1), kind=kOutput, calls=%fused_computation.21 | convolution fusion | flops 2151677952 | bytes 20971520 | tf_op jit(solution)/shard_map/dot_general | solution.py:23
  299.4 45.0 %shard_map.86 = (bf16[1024,1024]{1,0:T(8,128)(2,1)S(1)}, bf16[1024,1024]{1,0:T(8,128)(2,1)S(1)}) custom-call(f32[1024,1024]{1,0:T(8,128)S(1)} %add_subtract_fusion.gram_ref), custom_call_target="tpu_custom_call" | custom-call | flops 64424509440 | bytes 8388608 | tf_op jit(solution)/shard_map/pallas_call | solution.py:159
  344.4 4.7 %add_add_fusion = f32[1024,1024]{1,0:T(8,128)S(1)} fusion(f32[1024,1024]{1,0:T(8,128)} %fusion.46, f32[1024,1024]{1,0:T(8,128)S(1)} %fusion.42, bf16[1024,1024]{1,0:T(8,128)(2,1)S(1)} %get-tuple-element.17, f32[1024,1024]{1,0:T(8,128)S(1)} %add_add_fusion.1), kind=kOutput, calls=%fused_computation.20 | convolution fusion | flops 2150629376 | bytes 18874368 | tf_op jit(solution)/shard_map/dot_general | solution.py:23
  349.1 2.4 fusion.35
  351.4 2.3 fusion.14
  353.8 2.7 fusion.52
  356.6 1.3 fusion.10
  357.9 12.2 %fusion.12 = f32[2048,1024]{1,0:T(8,128)} fusion(bf16[2048,2048]{0,1:T(8,128)(2,1)S(1)} %bitcast.39, bf16[1024,1024]{1,0:T(8,128)(2,1)S(1)} %get-tuple-element.19, bf16[1024,1024]{1,0:T(8,128)(2,1)S(1)} %get-tuple-element.21), kind=kOutput, calls=%fused_computation.29 | convolution fusion | flops 8598323200 | bytes 20971520 | tf_op jit(solution)/shard_map/dot_general | solution.py:23
  370.1 1.4 fusion.15
  371.5 0.2 copy-done.9
  371.7 14.0 %add_convert_fusion = bf16[2048,1024]{1,0:T(8,128)(2,1)} fusion(f32[2048,1024]{1,0:T(8,128)} %fusion.12, bf16[2048,2048]{0,1:T(8,128)(2,1)S(1)} %bitcast.39, bf16[1024,1024]{1,0:T(8,128)(2,1)S(1)} %get-tuple-element.18, bf16[1024,1024]{1,0:T(8,128)(2,1)S(1)} %copy-done.9), kind=kOutput, calls=%fused_computation.7 | convolution fusion | flops 8602517504 | bytes 25165824 | tf_op jit(solution)/shard_map/dot_general | solution.py:23
  385.7 16.9 %multiply_add_fusion = f32[2048,1024]{1,0:T(8,128)} fusion(f32[2048,1024]{1,0:T(8,128)} %param.9, bf16[2048,1024]{1,0:T(8,128)(2,1)S(1)} %copy-done.3, bf16[2048,1024]{1,0:T(8,128)(2,1)} %add_convert_fusion, bf16[2048,1024]{1,0:T(8,128)(2,1)} %add_convert_fusion.1), kind=kOutput, calls=%fused_computation.5 | convolution fusion | flops 8615100416 | bytes 29360128 | tf_op jit(solution)/shard_map/aos,aol->asl/dot_general | solution.py:330
  402.6 18.6 %divide_convert_fusion.1.clone.5 = bf16[2048,1024]{1,0:T(8,128)(2,1)} fusion(f32[2048,1024]{1,0:T(8,128)} %multiply_add_fusion, f32[2048,1024]{1,0:T(8,128)} %multiply_add_fusion.1, bf16[2048,1024]{1,0:T(8,128)(2,1)} %add_convert_fusion, bf16[2048,1024]{1,0:T(8,128)(2,1)} %add_convert_fusion.1), kind=kOutput, calls=%fused_computation.4.clone.clone.clone.clone.2 | convolution fusion | flops 8615100416 | bytes 29360128 | tf_op jit(solution)/shard_map/aos,aol->asl/dot_general | solution.py:333
  421.3 15.1 %multiply_reduce_fusion = (f32[]{:T(128)}, f32[2048,1024]{1,0:T(8,128)}) fusion(bf16[2048,1024]{1,0:T(8,128)(2,1)} %add_convert_fusion, bf16[2048,1024]{1,0:T(8,128)(2,1)S(1)} %copy-done.10, bf16[2048,1024]{1,0:T(8,128)(2,1)} %divide_convert_fusion.1.clone.5), kind=kOutput, calls=%fused_computation.3 | convolution fusion | flops 8610906112 | bytes 20971524 | tf_op jit(solution)/shard_map/rfu,rup->rfp/dot_general | solution.py:340
  436.3 1.2 broadcast_in_dim.3.value_ref
  437.5 10.8 %shard_map.87 = f32[8,128]{1,0:T(8,128)} custom-call(f32[8,128]{1,0:T(8,128)} %broadcast_in_dim.3.value_ref), custom_call_target="tpu_custom_call" | custom-call | tf_op jit(solution)/shard_map/pallas_call | solution.py:286
  448.4 1.2 slice.22
  450.3 1.5 maximum_bitcast_fusion
  451.8 6.7 %multiply_convert_fusion = bf16[2048,1024]{1,0:T(8,128)(2,1)} fusion(f32[2048,1024]{1,0:T(8,128)} %get-tuple-element.25, f32[]{:T(128)} %bitcast.3), kind=kLoop, calls=%fused_computation.2 | loop fusion | flops 4194304 | bytes 12582916 | tf_op jit(solution)/shard_map/convert_element_type | solution.py:346
  (27 shorter events, 0.1 us)
Async XLA Ops:
  7.2 146.5 %all-gather.3.cloned.1.call-start = ((), (), s32[]{:S(2)}) async-start(), calls=%async_computation | async-start | bytes 10616832 | tf_op jit(solution)/shard_map/all_gather | solution.py:315
  12.9 221.5 %all-gather.5.cloned.1.call-start = ((), (), s32[]{:S(2)}) async-start(), calls=%async_computation.1 | async-start | bytes 4718592 | tf_op jit(solution)/shard_map/all_gather | solution.py:320
  159.0 13.0 %copy-start = (bf16[2048,2048]{1,0:T(8,128)(2,1)}, bf16[2048,2048]{1,0:T(8,128)(2,1)S(1)}, u32[]{:S(2)}) copy-start(bf16[2048,2048]{1,0:T(8,128)(2,1)S(1)} %shard_map.84) | copy-start | bytes 25165828
  172.0 2.0 copy-start.5
  178.5 45.0 %copy-start.6 = (bf16[2048,1024]{0,1:T(8,128)(2,1)S(1)}, bf16[2048,1024]{0,1:T(8,128)(2,1)}, u32[]{:S(2)}) copy-start(bf16[2048,1024]{0,1:T(8,128)(2,1)} %copy-done.5) | copy-start | bytes 12582916
  223.5 4.6 copy-start.1
  265.0 2.4 copy-start.2
  281.3 2.6 copy-start.7
  351.4 5.1 %slice-start = ((s8[8388608]{0:T(1024)(128)(4,1)}), s8[4194304]{0:T(1024)(128)(4,1)S(1)}, s32[]{:S(2)}) async-start(s8[8388608]{0:T(1024)(128)(4,1)} %bitcast.38), calls=%async_computation.2 | async-start | bytes 8388608
  353.8 2.8 slice-start.1
  356.5 1.4 copy-start.8
  370.1 1.6 copy-start.9
  371.7 14.0 %copy-start.3 = (bf16[2048,1024]{1,0:T(8,128)(2,1)S(1)}, bf16[2048,1024]{1,0:T(8,128)(2,1)}, u32[]{:S(2)}) copy-start(bf16[2048,1024]{1,0:T(8,128)(2,1)} %param.7) | copy-start | bytes 12582916
  402.6 18.7 %copy-start.10 = (bf16[2048,1024]{1,0:T(8,128)(2,1)S(1)}, bf16[2048,1024]{1,0:T(8,128)(2,1)}, u32[]{:S(2)}) copy-start(bf16[2048,1024]{1,0:T(8,128)(2,1)} %add_convert_fusion.1) | copy-start | bytes 12582916
  421.3 29.0 %copy-start.4 = (f32[256,1024]{1,0:T(8,128)S(1)}, f32[256,1024]{1,0:T(8,128)}, u32[]{:S(2)}) copy-start(f32[256,1024]{1,0:T(8,128)} %convolution_add_fusion) | copy-start | bytes 3145732
Sparse Core Ops, SparseCore 0:
  13.0 140.5 all-gather.2
  156.3 71.5 all-gather.4
